TPU v7x, 256 devices: a whole 4x4x8 slice. The times are simulated.
256 devices in a mesh: spin: 2 (over core), band: 128 (over y, z, x).
Axes of the slice: x: 4, y: 4, z: 8, core: 2. Of those that a mesh axis runs over, the one named last changes fastest.
Arguments:
- orbitals: float32 [2, 128, 32768], P('spin', 'band'), may hold values from -15 to 15
- potential: float32 [32768], replicated, may hold values from -6 to 6
Outputs:
- updated: float32 [2, 128, 32768], P('spin', 'band')
- residual: float32 [2, 128, 32768], P('spin', 'band')
All inputs are finite; a program needn't handle non-finite values.
Results may differ from a plain program's by a relative error of at most 0.0003.
Values sent between devices are 32-bit elements; how exact they have to be, the bound alone decides.
No kernel may reach another device: no remote copies, remote signals or barrier semaphores. Data moves between devices by JAX's collectives and lax.ppermute only.
A program may use at most 128 MiB of HBM per device.

v0:
```python
import math

import jax
import jax.numpy as jnp
from jax import lax
from jax.sharding import PartitionSpec as P

GRID = 32


screen_square = 0.04
hartree_weight = 0.03125
mixing = 0.25
step_length = 0.1


def passed_along(x, axis, by):
    peers = lax.axis_size(axis)
    return lax.ppermute(x, axis, [(i, (i + by) % peers) for i in range(peers)])


def cas_table(points):
    indices = jnp.arange(points, dtype=jnp.int32)
    phase_index = indices[:, None] * indices[None, :] % points
    angles = phase_index.astype(jnp.float32) * (2.0 * math.pi / points)
    return jnp.cos(angles) + jnp.sin(angles)


def wave_squares(points):
    indices = jnp.arange(points, dtype=jnp.int32)
    folded = jnp.where(indices < points // 2, indices, indices - points).astype(jnp.float32)
    wavenumber = folded * (math.pi / points)
    squares = wavenumber * wavenumber
    summed = squares[:, None, None] + squares[None, :, None] + squares[None, None, :]
    return summed.reshape(-1)


def plane_table(table):
    points = table.shape[0]
    joined = table[:, None, :, None] * table[None, :, None, :]
    return joined.reshape(points * points, points * points)


def hartley(signal, tables):
    table, joined = tables
    points = table.shape[0]
    leading = signal.shape[:-1]
    planes = signal.reshape((-1, points, points * points))
    planes = jnp.einsum("ka,sar->skr", table, planes, precision=lax.Precision.HIGHEST)
    planes = jnp.einsum("sar,qr->saq", planes, joined, precision=lax.Precision.HIGHEST)
    return planes.reshape(leading + (points**3,))


def screened(signal, tables, kernel):
    return hartley(kernel * hartley(signal, tables), tables) / kernel.shape[0]


def correlation(left_rows, right_rows):
    product = lax.dot_general(
        left_rows, right_rows, (((1,), (1,)), ((), ())), precision=lax.Precision.HIGHEST
    )
    return product / (left_rows.shape[1] * lax.axis_size("band"))


def remove(values, weights, basis):
    return values - lax.dot_general(
        weights, basis, (((0,), (0,)), ((), ())), precision=lax.Precision.HIGHEST
    )


def per_device(orbitals, potential):
    table = cas_table(GRID)
    tables = (table, plane_table(table))
    wave_square = wave_squares(GRID)
    kernel = jnp.where(wave_square > 0, 1.0 / (wave_square + screen_square), 0.0)
    volume = orbitals.shape[2]
    density = lax.psum(jnp.sum(orbitals * orbitals, axis=(0, 1)), ("spin", "band"))
    local_field = potential + hartree_weight * screened(density, tables, kernel)
    resident = orbitals[0]
    band_count = resident.shape[0]

    def pair_terms(left_rows, right_rows):
        pair_field = (left_rows[:, None, :] * right_rows[None, :, :]).reshape(-1, volume)
        return screened(pair_field, tables, kernel).reshape(band_count, band_count, volume)

    exchange_term = -jnp.sum(pair_terms(resident, resident) * resident[None, :, :], axis=1)
    for offset in (1, 2, -1, -2):
        partner = passed_along(resident, "band", offset)
        fields = pair_terms(resident, partner)
        exchange_term = exchange_term - jnp.sum(fields * partner[None, :, :], axis=1)
    kinetic = hartley(0.5 * wave_square * hartley(resident, tables), tables) / volume
    gradient = kinetic + local_field * resident + mixing * exchange_term

    def project(values):
        orbital_slab, value_slab = (
            lax.all_to_all(resident, "band", split_axis=1, concat_axis=0, tiled=True),
            lax.all_to_all(values, "band", split_axis=1, concat_axis=0, tiled=True),
        )
        weights = lax.psum(correlation(orbital_slab, value_slab), "band")
        return lax.all_to_all(
            remove(value_slab, weights, orbital_slab),
            "band",
            split_axis=0,
            concat_axis=1,
            tiled=True,
        )

    residual = project(project(gradient))
    return ((resident - step_length * residual)[None], residual[None])


def solution(mesh):
    return jax.shard_map(
        per_device,
        mesh=mesh,
        in_specs=(P("spin", "band", None), P()),
        out_specs=(P("spin", "band", None), P("spin", "band", None)),
        check_vma=False,
    )
```

profile of v0, /device:TPU:2, one launch (start us, length us, event | category | flops | bytes accessed | tf_op | source)
XLA Modules:
  0.0 821.0 jit_solution(12687801225815517972)
XLA Ops:
  7.2 9.9 %collective-permute-start.3 = (f32[1,32768]{1,0:T(1,128)}, f32[1,32768]{1,0:T(1,128)S(1)}, u32[]{:S(2)}, u32[]{:S(2)}) collective-permute-start(f32[1,32768]{1,0:T(1,128)} %bitcast.194), channel_id=1, source_target_pairs={{0,126},{1,127},{2,0},{3,1},{4,2},{5,3},{6,4},{7,5},{8,6},{9,7},{1... | collective-permute-start | bytes 393224 | tf_op jit(solution)/shard_map/ppermute | solution.py:19
  17.1 1.4 collective-permute-start.2
  19.1 12.4 %all-to-all-start.1 = ((f32[1,128,256]{2,0,1:T(1,128)}), f32[1,128,256]{2,0,1:T(1,128)S(1)}, u32[]{:S(2)}, u32[]{:S(2)}) async-start(f32[1,128,256]{2,0,1:T(1,128)} %bitcast.198), calls=%async_computation.1 | async-start | bytes 262144 | tf_op jit(solution)/shard_map/all_to_all | solution.py:96
  31.6 8.0 broadcast_multiply_fusion
  39.6 13.7 %mul.632 = f32[1024,1024]{1,0:T(8,128)} reshape(f32[32,32,32,32]{3,2,1,0:T(8,128)} %broadcast_multiply_fusion) | data formatting | bytes 8388608 | tf_op jit(solution)/shard_map/mul | solution.py:40
  54.5 2.6 fusion.92
  58.9 6.2 convolution_multiply_fusion.9
  65.1 3.9 convolution_multiply_fusion.1
  69.4 3.9 fusion
  73.7 6.6 convolution_multiply_fusion.3
  80.7 3.9 fusion.1
  85.1 6.2 convolution_multiply_fusion.5
  91.7 3.9 fusion.2
  96.0 4.1 convolution_multiply_fusion.8
  100.8 6.2 convolution_multiply_fusion.7
  107.4 3.9 fusion.3
  111.7 6.2 convolution_multiply_fusion.13
  118.3 4.1 fusion.5
  122.6 185.5 %all-reduce.4.cloned.1.call-done = f32[32,1024]{1,0:T(8,128)} async-done(((f32[32,1024]{1,0:T(8,128)}), f32[32,1024]{1,0:T(8,128)}) %all-reduce.4.cloned.1.call-update) | async-done | bytes 131088 | tf_op jit(solution)/shard_map/psum | solution.py:77
  308.2 1.4 convolution_bitcast_fusion.11
  309.6 6.1 convolution_multiply_fusion.11
  316.0 3.9 fusion.4
  320.1 20.5 %all_to_all.82 = f32[1,128,256]{2,0,1:T(1,128)S(1)} all-to-all(f32[1,128,256]{2,0,1:T(1,128)S(1)} %bitcast.208), channel_id=1, replica_groups=mesh['spin'=2,'band'=128] {'band'}, dimensions={1} | all-to-all | bytes 262144 | tf_op jit(solution)/shard_map/all_to_all | solution.py:97
  340.6 0.9 fusion.9
  341.6 203.6 %all-reduce.6.cloned.1.call-done = f32[128,128]{0,1:T(8,128)} async-done(((f32[128,128]{0,1:T(8,128)}), f32[128,128]{0,1:T(8,128)}) %all-reduce.6.cloned.1.call-update) | async-done | bytes 65552 | tf_op jit(solution)/shard_map/psum | solution.py:99
  545.2 1.1 fusion.7
  546.5 21.3 %all_to_all.83 = f32[128,1,256]{2,1,0:T(1,128)S(1)} all-to-all(f32[128,1,256]{2,1,0:T(1,128)S(1)} %copy.4), channel_id=1, replica_groups=mesh['spin'=2,'band'=128] {'band'}, dimensions={0} | all-to-all | bytes 262144 | tf_op jit(solution)/shard_map/all_to_all | solution.py:100
  567.8 17.8 %all_to_all.84 = f32[1,128,256]{2,0,1:T(1,128)S(1)} all-to-all(f32[1,128,256]{2,0,1:T(1,128)S(1)} %bitcast.214), channel_id=1, replica_groups=mesh['spin'=2,'band'=128] {'band'}, dimensions={1} | all-to-all | bytes 262144 | tf_op jit(solution)/shard_map/all_to_all | solution.py:97
  585.7 0.9 fusion.8
  586.6 203.4 %all-reduce.8.cloned.1.call-done = f32[128,128]{0,1:T(8,128)} async-done(((f32[128,128]{0,1:T(8,128)}), f32[128,128]{0,1:T(8,128)}) %all-reduce.8.cloned.1.call-update) | async-done | bytes 65552 | tf_op jit(solution)/shard_map/psum | solution.py:99
  790.0 1.1 fusion.6
  791.2 21.3 %all_to_all.85 = f32[128,1,256]{2,1,0:T(1,128)S(1)} all-to-all(f32[128,1,256]{2,1,0:T(1,128)S(1)} %copy.5), channel_id=1, replica_groups=mesh['spin'=2,'band'=128] {'band'}, dimensions={0} | all-to-all | bytes 262144 | tf_op jit(solution)/shard_map/all_to_all | solution.py:100
  (71 shorter events, 10.0 us)
Async XLA Ops:
  7.2 46.8 %collective-permute-start.3 = (f32[1,32768]{1,0:T(1,128)}, f32[1,32768]{1,0:T(1,128)S(1)}, u32[]{:S(2)}, u32[]{:S(2)}) collective-permute-start(f32[1,32768]{1,0:T(1,128)} %bitcast.194), channel_id=1, source_target_pairs={{0,126},{1,127},{2,0},{3,1},{4,2},{5,3},{6,4},{7,5},{8,6},{9,7},{1... | collective-permute-start | bytes 393224 | tf_op jit(solution)/shard_map/ppermute | solution.py:19
  17.1 36.8 %collective-permute-start.2 = (f32[1,32768]{1,0:T(1,128)}, f32[1,32768]{1,0:T(1,128)S(1)}, u32[]{:S(2)}, u32[]{:S(2)}) collective-permute-start(f32[1,32768]{1,0:T(1,128)} %bitcast.195), channel_id=1, source_target_pairs={{0,127},{1,0},{2,1},{3,2},{4,3},{5,4},{6,5},{7,6},{8,7},{9,8},{10,... | collective-permute-start | bytes 393224 | tf_op jit(solution)/shard_map/ppermute | solution.py:19
  18.5 35.4 %collective-permute-start.1 = (f32[1,32768]{1,0:T(1,128)}, f32[1,32768]{1,0:T(1,128)S(1)}, u32[]{:S(2)}, u32[]{:S(2)}) collective-permute-start(f32[1,32768]{1,0:T(1,128)} %bitcast.196), channel_id=1, source_target_pairs={{0,2},{1,3},{2,4},{3,5},{4,6},{5,7},{6,8},{7,9},{8,10},{9,11},{10,... | collective-permute-start | bytes 393224 | tf_op jit(solution)/shard_map/ppermute | solution.py:19
  18.5 35.4 %collective-permute-start = (f32[1,32768]{1,0:T(1,128)}, f32[1,32768]{1,0:T(1,128)S(1)}, u32[]{:S(2)}, u32[]{:S(2)}) collective-permute-start(f32[1,32768]{1,0:T(1,128)} %bitcast.197), channel_id=1, source_target_pairs={{0,1},{1,2},{2,3},{3,4},{4,5},{5,6},{6,7},{7,8},{8,9},{9,10},{10,1... | collective-permute-start | bytes 393224 | tf_op jit(solution)/shard_map/ppermute | solution.py:19
  19.1 301.0 %all-to-all-start.1 = ((f32[1,128,256]{2,0,1:T(1,128)}), f32[1,128,256]{2,0,1:T(1,128)S(1)}, u32[]{:S(2)}, u32[]{:S(2)}) async-start(f32[1,128,256]{2,0,1:T(1,128)} %bitcast.198), calls=%async_computation.1 | async-start | bytes 262144 | tf_op jit(solution)/shard_map/all_to_all | solution.py:96
  39.6 14.9 %copy-start.6 = (f32[1,1,32768]{2,1,0:T(1,128)S(1)}, f32[1,1,32768]{2,1,0:T(1,128)}, u32[]{:S(2)}) copy-start(f32[1,1,32768]{2,1,0:T(1,128)} %param.2) | copy-start | bytes 393220
  57.5 0.7 copy-start.7
  57.9 250.3 %all-reduce.4.cloned.1.call-start = ((), (), s32[]{:S(2)}) async-start(), calls=%async_computation.5 | async-start | bytes 262144 | tf_op jit(solution)/shard_map/psum | solution.py:77
  58.6 486.6 %all-reduce.6.cloned.1.call-start = ((), (), s32[]{:S(2)}) async-start(), calls=%async_computation.6 | async-start | bytes 131072 | tf_op jit(solution)/shard_map/psum | solution.py:99
  58.9 6.2 copy-start
  73.4 7.3 copy-start.1
  84.7 7.0 copy-start.2
  100.4 7.0 copy-start.3
  111.4 7.0 copy-start.4
  308.2 7.8 copy-start.5
  309.6 10.4 %copy-start.8 = (f32[32768]{0:T(1024)S(1)}, f32[32768]{0:T(1024)}, u32[]{:S(2)}) copy-start(f32[32768]{0:T(1024)} %param.3) | copy-start | bytes 393220
  341.6 448.4 %all-reduce.8.cloned.1.call-start = ((), (), s32[]{:S(2)}) async-start(), calls=%async_computation.7 | async-start | bytes 131072 | tf_op jit(solution)/shard_map/psum | solution.py:99
Sparse Core Ops, SparseCore 0:
  64.8 243.3 all-reduce.3
  341.7 203.5 all-reduce.5
  586.7 203.2 all-reduce.7
where the time goes:
time: 829 us; the launch traced here: 821 us
  waiting for transfers between devices  593 us (72%)
  blocking collectives  81 us (10%)
  matrix products  79.3 us (10%)
  starting transfers between devices  24.7 us (3%)
  local copies, waits for them, and re-layouts  16.4 us (2%)
  between operations  14.7 us (2%)
  other arithmetic  11.9 us (1%)
    psum x2, waiting for transfers between devices, project(): weights = lax.psum(correlation(orbital_slab, value_slab), 'band')  407 us
    psum x1, waiting for transfers between devices, per_device(): lax.psum(jnp.sum(orbitals * orbitals, axis=(0, 1)), ('spin', 'band'))  186 us
    dot_general x14, matrix products, hartley(): jnp.einsum('sar,qr->saq', planes, joined, precision=lax.Precision.HIGHEST)  69.3 us
    all_to_all x2, blocking collectives, project(): lax.all_to_all(remove(value_slab, weights, orbital_slab), 'band', split_a...  42.7 us
    all_to_all x2, blocking collectives, project(): lax.all_to_all(values, 'band', split_axis=1, concat_axis=0, tiled=True)  38.3 us
  transfers between devices with their start and end apart: 8, of which 3 were waited for; matrix products, arithmetic and copies ran while one was open for 12% of the time, Pallas kernels for 0%

commit v1 on v0

v1 whole, which is shorter than its diff:
```python
import math

import jax
import jax.numpy as jnp
import ml_dtypes
import numpy as np
from jax import lax
from jax.experimental import pallas as pl
from jax.experimental.pallas import tpu as pltpu
from jax.sharding import Mesh
from jax.sharding import PartitionSpec as P

GRID = 32
PLANE = GRID * GRID
CELLS = GRID**3
LANES = 128
ROWS = CELLS // LANES
SPLIT = PLANE // LANES

SCREEN_SQUARE = 0.04
HARTREE_WEIGHT = 0.03125
MIXING = 0.25
STEP_LENGTH = 0.1

BANDS = ("y", "z", "x")
GRID_X = 4
SLAB = ("y", "x")
GATHER = ("z",)

f32 = jnp.float32
bf16 = jnp.bfloat16


def halves(value):
    high = value.astype(ml_dtypes.bfloat16)
    low = (value - high.astype(np.float64)).astype(ml_dtypes.bfloat16)
    return high, low


def constants():
    indices = np.arange(GRID)
    angles = (indices[:, None] * indices[None, :] % GRID) * (2.0 * math.pi / GRID)
    table = np.cos(angles) + np.sin(angles)
    joined = np.stack(halves(np.kron(table, table)))
    lines = np.stack(halves(np.kron(np.eye(4), table)))
    return jnp.asarray(joined), jnp.asarray(lines)


def wave_square():
    planes = lax.broadcasted_iota(jnp.int32, (GRID, PLANE), 0)
    cells = lax.broadcasted_iota(jnp.int32, (GRID, PLANE), 1)

    def square(index):
        wave = jnp.where(index < GRID // 2, index, index - GRID).astype(f32) * (math.pi / GRID)
        return wave * wave

    return square(planes) + square(cells // GRID) + square(cells % GRID)


def screening(squares):
    kept = squares > 0
    return jnp.where(kept, 1.0 / jnp.where(kept, squares + SCREEN_SQUARE, 1.0), 0.0) * (1.0 / CELLS)


def split(value):
    high = value.astype(bf16)
    return high, (value - high.astype(f32)).astype(bf16)


def mm(left, right):
    return lax.dot_general(left, right, (((1,), (0,)), ((), ())), preferred_element_type=f32)


def mmt(left, right):
    return lax.dot_general(left, right, (((1,), (1,)), ((), ())), preferred_element_type=f32)


def product(left, right_high, right_low, multiply):
    high, low = split(left)
    rows = left.shape[0]
    both = multiply(jnp.concatenate([high, low], axis=0), right_high)
    return both[:rows] + both[rows:] + multiply(high, right_low)


def along_line(value, lines):
    rows = value.shape[0]
    line_high, line_low = lines[0, :rows, :rows], lines[1, :rows, :rows]
    high, low = split(value)
    both = mm(jnp.concatenate([line_high, line_low], axis=0), high)
    return both[:rows] + both[rows:] + mm(line_high, low)


def twice_transformed(fields, factors, joined, lines, copies):
    high, low = split(fields)
    rows = fields.shape[0]
    copies[0].wait()
    both = mm(jnp.concatenate([high, low], axis=0), joined[0])
    copies[1].wait()
    value = both[:rows] + both[rows:] + mm(high, joined[1])
    copies[2].wait()
    value = along_line(value, lines) * factors
    return along_line(product(value, joined[0], joined[1], mm), lines)


def to_planes(ref):
    return jnp.concatenate([ref[pl.ds(j, GRID, stride=SPLIT), :] for j in range(SPLIT)], axis=1)


def table_copies(joined_ref, lines_ref, joined, lines, sems):
    copies = [
        pltpu.make_async_copy(joined_ref.at[0], joined.at[0], sems.at[0]),
        pltpu.make_async_copy(joined_ref.at[1], joined.at[1], sems.at[1]),
        pltpu.make_async_copy(lines_ref, lines, sems.at[2]),
    ]
    for copy in copies:
        copy.start()
    return copies


TABLE_SCRATCH = [
    pltpu.VMEM((2, PLANE, PLANE), bf16),
    pltpu.VMEM((2, LANES, LANES), bf16),
    pltpu.SemaphoreType.DMA((3,)),
]


def own_kernel(o_ref, joined_ref, lines_ref, square_ref, start_ref, joined, lines, sems):
    copies = table_copies(joined_ref, lines_ref, joined, lines, sems)
    own = to_planes(o_ref)
    fields = jnp.concatenate([own * own, own], axis=0)
    squares = wave_square()
    factors = jnp.concatenate([screening(squares), squares * (0.5 / CELLS)], axis=0)
    fields = twice_transformed(fields, factors, joined, lines, copies)
    square, kinetic = fields[:GRID], fields[GRID:]
    start = kinetic - MIXING * square * own
    for j in range(SPLIT):
        rows = pl.ds(j, GRID, stride=SPLIT)
        start_ref[rows, :] = start[:, j * LANES : (j + 1) * LANES]
        square_ref[rows, :] = square[:, j * LANES : (j + 1) * LANES]


def pack_kernel(o_ref, square_ref, other_ref, packed_ref):
    shape = packed_ref.shape[0], packed_ref.shape[2], LANES
    packed_ref[:, 0] = o_ref[...].reshape(shape)
    packed_ref[:, 1] = (square_ref[...] + other_ref[...]).reshape(shape)


def pair_kernel(x_ref, o_ref, start_ref, below, above, second, across, corner, joined_ref, lines_ref, out_ref, joined, lines, sems):
    copies = table_copies(joined_ref, lines_ref, joined, lines, sems)
    own = to_planes(o_ref)
    below, above, second, across, corner = (to_planes(ref) for ref in (below, above, second, across, corner))
    x = x_ref[0]
    partners = [
        jnp.where(x == 0, corner, below),
        jnp.where(x == GRID_X - 1, corner, above),
        second,
        across,
    ]
    fields = jnp.concatenate([own * partner for partner in partners], axis=0)
    factors = jnp.concatenate([screening(wave_square())] * 4, axis=0)
    fields = twice_transformed(fields, factors, joined, lines, copies)
    total = sum(fields[k * GRID : (k + 1) * GRID] * partners[k] for k in range(4))
    for j in range(SPLIT):
        rows = pl.ds(j, GRID, stride=SPLIT)
        out_ref[rows, :] = start_ref[rows, :] - MIXING * total[:, j * LANES : (j + 1) * LANES]


def slab_kernel(slabs_ref, out_ref):
    bands, rows = slabs_ref.shape[0], slabs_ref.shape[2]
    out_ref[: bands * rows] = slabs_ref[:, 0].reshape(bands * rows, LANES)
    out_ref[bands * rows :] = jnp.sum(slabs_ref[:, 1], axis=0)


def correlate_kernel(g_ref, potential_ref, *refs):
    pieces, (corr_ref, g_out, oh_ref, ol_ref) = refs[:-4], refs[-4:]
    bands, rows = g_ref.shape[0], g_ref.shape[1]
    cells = bands * rows
    count = bands * len(pieces)
    squares = sum(piece[cells:, :] for piece in pieces)
    local = potential_ref[...] + HARTREE_WEIGHT * squares
    g = g_ref[...] + local[None] * pieces[0][:cells].reshape(bands, rows, LANES)
    g_out[...] = g
    for k, piece in enumerate(pieces):
        for c in range(rows):
            high, low = split(piece[pl.ds(c, bands, stride=rows), :])
            oh_ref[k * bands : (k + 1) * bands, c * LANES : (c + 1) * LANES] = high
            ol_ref[k * bands : (k + 1) * bands, c * LANES : (c + 1) * LANES] = low
    wide = jnp.concatenate([g[:, c, :] for c in range(rows)], axis=1)
    g_high, g_low = split(wide)
    high, low = oh_ref[...], ol_ref[...]
    left_high = jnp.concatenate([g_high, high], axis=0)
    left_low = jnp.concatenate([g_low, low], axis=0)
    total = mmt(left_high, high) + mmt(left_low, high) + mmt(left_high, low)
    total = total * (1.0 / CELLS)
    half = count // 2
    quarter = half // 2
    kept = bands + half
    corner = total[kept:, half:]
    corr_ref[:kept] = total[:kept]
    corr_ref[kept:] = jnp.concatenate([corner[:quarter], corner[quarter:]], axis=1)


def remove_kernel(corr_ref, g_ref, oh_ref, ol_ref, out_ref):
    bands, rows = g_ref.shape[0], g_ref.shape[1]
    corr = jnp.sum(corr_ref[...], axis=0)
    half = corr.shape[1] // 2
    kept = bands + half
    first, upper, corner = corr[:bands], corr[bands:kept], corr[kept:]
    lower = jnp.concatenate([corner[:, :half], corner[:, half:]], axis=0)
    lower = jnp.concatenate([upper[:, half:].T, lower], axis=1)
    overlap = jnp.concatenate([upper, lower], axis=0)
    s_high, s_low = split(overlap)
    weights = 2.0 * first - product(first, s_high, s_low, mm)
    taken = product(weights, oh_ref[...], ol_ref[...], mm)
    for c in range(rows):
        out_ref[:, c, :] = g_ref[:, c, :] - taken[:, c * LANES : (c + 1) * LANES]


def call(kernel, outs, args, name, tables=(), flops=1 << 30, nbytes=1 << 23):
    single = not isinstance(outs, list)
    shapes = [outs] if single else outs
    result = pl.pallas_call(
        kernel,
        out_shape=[jax.ShapeDtypeStruct(s, t) for s, t in shapes],
        in_specs=[pl.BlockSpec(memory_space=pltpu.SMEM if a.dtype == jnp.int32 else pltpu.VMEM) for a in args]
        + [pl.BlockSpec(memory_space=pltpu.HBM)] * len(tables),
        out_specs=[pl.BlockSpec(memory_space=pltpu.VMEM)] * len(shapes),
        compiler_params=pltpu.CompilerParams(vmem_limit_bytes=40 << 20),
        cost_estimate=pl.CostEstimate(flops=flops, bytes_accessed=nbytes, transcendentals=0),
        scratch_shapes=TABLE_SCRATCH if tables else [],
        name=name,
    )(*args, *tables)
    return result[0] if single else result


def exchange(x, axes):
    return lax.all_to_all(x, axes, 0, 0, tiled=True)


def gather(x, axes):
    return exchange(jnp.broadcast_to(x[None], (size(axes),) + x.shape), axes)


def size(axes):
    return math.prod(lax.axis_size(a) for a in axes)


def shifted(x, axes, by):
    peers = size(axes)
    return lax.ppermute(x, axes, [(i, (i + by) % peers) for i in range(peers)])


def per_device(orbitals, potential):
    tables = constants()
    parts = size(SLAB)
    rows = ROWS // parts
    groups = size(GATHER)

    own = orbitals.reshape(ROWS, LANES)
    below, above, second = (shifted(own, ("x",), by) for by in (1, -1, 2))
    rings = size(("y", "z"))
    toward = [-1, -1, 1, 1]
    edge = lax.ppermute(
        own,
        BANDS,
        [(g * GRID_X + x, (g + toward[x]) % rings * GRID_X + x) for g in range(rings) for x in range(GRID_X)],
    )
    square, start = call(
        own_kernel,
        [((ROWS, LANES), f32), ((ROWS, LANES), f32)],
        [own],
        "own_fields",
        tables,
    )
    other = shifted(square, ("spin",), 1)
    packed = call(pack_kernel, ((parts, 2, rows, LANES), f32), [own, square, other], "pack")
    packed, start, edge, below, above, second = lax.optimization_barrier((packed, start, edge, below, above, second))
    across = shifted(edge, ("x",), 2)
    corner = lax.ppermute(edge, "x", [(0, GRID_X - 1), (GRID_X - 1, 0)])
    slabs = exchange(packed, SLAB)
    slab = call(slab_kernel, (((parts + 1) * rows, LANES), f32), [slabs], "slab")
    pieces = [slab] + [shifted(slab, GATHER, by) for by in (1, -1, 2, -2, 3, -3, 4)]
    gradient = call(
        pair_kernel,
        ((ROWS, LANES), f32),
        [lax.axis_index("x").reshape(1), own, start, below, above, second, across, corner],
        "pair_fields",
        tables,
    )
    gradient, slab = lax.optimization_barrier((gradient, slab))
    slab_gradient = exchange(gradient.reshape(parts, rows, LANES), SLAB)
    here = lax.axis_index(SLAB)
    slab_potential = lax.dynamic_slice_in_dim(potential.reshape(ROWS, LANES), here * rows, rows, 0)
    bands = parts * groups
    corr, slab_gradient, o_high, o_low = call(
        correlate_kernel,
        [
            ((parts + 3 * bands // 4, LANES), f32),
            ((parts, rows, LANES), f32),
            ((bands, rows * LANES), bf16),
            ((bands, rows * LANES), bf16),
        ],
        [slab_gradient, slab_potential, *pieces],
        "correlations",
    )
    spread = gather(corr, SLAB)
    slab_residual = call(
        remove_kernel,
        ((parts, rows, LANES), f32),
        [spread, slab_gradient, o_high, o_low],
        "removal",
    )
    residual = exchange(slab_residual, SLAB).reshape(1, 1, CELLS)
    return orbitals - STEP_LENGTH * residual, residual


def solution(mesh):
    fine = Mesh(mesh.devices.reshape(2, 4, 8, 4), ("spin",) + BANDS)
    spec = P("spin", BANDS, None)
    return jax.shard_map(
        per_device, mesh=fine, in_specs=(spec, P()), out_specs=(spec, spec), check_vma=False
    )
```

time: 829 us -> 108 us (0.13)
  waiting for transfers between devices: 593 us -> 10.6 us
  matrix products: 79.3 us -> 0 us
  blocking collectives: 81 us -> 41.5 us
  between operations: 14.7 us -> 0.79 us
  starting transfers between devices: 24.7 us -> 38.6 us
  other arithmetic: 11.9 us -> 0.84 us
  local copies, waits for them, and re-layouts: 16.4 us -> 6.9 us
    psum x3 -> x0, waiting for transfers between devices: 593 us -> none  [the longest x2 407 us: project(): weights = lax.psum(correlation(orbital_slab, value_slab), 'band')]
    dot_general x32 -> x0, matrix products: 79.3 us -> none  [the longest x14 69.3 us: hartley(): jnp.einsum('sar,qr->saq', planes, joined, precision=lax.Precision.HIGHEST)]
    all_to_all x4 -> x3, blocking collectives: 81 us -> 41.5 us  [exchange(): return lax.all_to_all(x, axes, 0, 0, tiled=True)]
    ppermute x4 -> x14, starting transfers between devices: 12 us -> 32.5 us  [the longest x12 23.6 us: shifted(): return lax.ppermute(x, axes, [(i, (i + by) % peers) for i in range(peers)])]
    mul x1 -> x0, local copies, waits for them, and re-layouts: 13.7 us -> none  [plane_table(): joined = table[:, None, :, None] * table[None, :, None, :]]
  transfers between devices with their start and end apart: 8 -> 15, of which waited for: 3 -> 3; matrix products, arithmetic and copies ran while one was open for 12% -> 0% of each run, Pallas kernels for 0% -> 4%
where the time goes in v1:
time: 108 us; the launch traced here: 107 us
  blocking collectives  41.5 us (38%)
  starting transfers between devices  38.6 us (36%)
  waiting for transfers between devices  10.6 us (10%)
  Pallas kernels  8.16 us (8%)
  local copies, waits for them, and re-layouts  6.9 us (6%)
    all_to_all x3, blocking collectives, exchange(): return lax.all_to_all(x, axes, 0, 0, tiled=True)  41.5 us
    ppermute x12, starting transfers between devices, shifted(): return lax.ppermute(x, axes, [(i, (i + by) % peers) for i in range(peers)])  23.6 us
    ppermute x1, starting transfers between devices, per_device(): lax.ppermute(own, BANDS, [(g * GRID_X + x, (g + toward[x]) % rings * GRID...  8.31 us
    pallas_call x6, Pallas kernels, call(): pl.pallas_call(kernel, out_shape=[jax.ShapeDtypeStruct(s, t) for s, t in...  8.16 us
    unnamed x15, local copies, waits for them, and re-layouts  6.83 us
    all_to_all x1, waiting for transfers between devices, exchange(): return lax.all_to_all(x, axes, 0, 0, tiled=True)  6.69 us
    all_to_all x1, starting transfers between devices, exchange(): return lax.all_to_all(x, axes, 0, 0, tiled=True)  6.03 us
    ppermute x1, waiting for transfers between devices, per_device(): lax.ppermute(own, BANDS, [(g * GRID_X + x, (g + toward[x]) % rings * GRID...  2.46 us
  transfers between devices with their start and end apart: 15, of which 3 were waited for; matrix products, arithmetic and copies ran while one was open for 0% of the time, Pallas kernels for 4%

profile of v1, /device:TPU:2, one launch (start us, length us, event | category | flops | bytes accessed | tf_op | source)
XLA Modules:
  0.0 107.3 jit_solution(17352287896199277703)
XLA Ops:
  0.6 0.0 copy-start
  0.7 2.2 %copy-done.1 = bf16[2,1024,1024]{2,1,0:T(8,128)(2,1)S(1)} copy-done((bf16[2,1024,1024]{2,1,0:T(8,128)(2,1)S(1)}, bf16[2,1024,1024]{2,1,0:T(8,128)(2,1)}, u32[]{:S(2)}) %copy-start.1) | copy-done | bytes 4194328
  2.9 0.9 copy-done.3
  3.8 0.8 copy-done.5
  4.6 2.5 %own_fields.1 = (f32[256,128]{1,0:T(8,128)S(1)}, f32[256,128]{1,0:T(8,128)S(1)}) custom-call(f32[256,128]{1,0:T(8,128)S(1)} %bitcast.6, bf16[2,1024,1024]{2,1,0:T(8,128)(2,1)S(1)} %copy-done.1, bf16[2,128,128]{2,1,0:T(8,128)(2,1)S(1)} %copy-done.5), custom_call_target="tpu_custom_call" | custom-call | flops 1073741824 | bytes 8388608 | tf_op jit(solution)/shard_map/own_fields/pallas_call | solution.py:222
  7.1 0.1 collective-permute-start
  7.2 2.2 %collective-permute-start.4 = (f32[256,128]{1,0:T(8,128)S(1)}, f32[256,128]{1,0:T(8,128)S(1)}, u32[]{:S(2)}, u32[]{:S(2)}) collective-permute-start(f32[256,128]{1,0:T(8,128)S(1)} %bitcast.7), channel_id=1, source_target_pairs={{0,2},{1,3},{2,0},{3,1},{4,6},{5,7},{6,4},{7,5},{8,10},{9,11},{10,... | collective-permute-start | bytes 393224 | tf_op jit(solution)/shard_map/ppermute | solution.py:250
  9.5 1.4 %collective-permute-start.3 = (f32[256,128]{1,0:T(8,128)S(1)}, f32[256,128]{1,0:T(8,128)S(1)}, u32[]{:S(2)}, u32[]{:S(2)}) collective-permute-start(f32[256,128]{1,0:T(8,128)S(1)} %bitcast.8), channel_id=1, source_target_pairs={{0,3},{1,0},{2,1},{3,2},{4,7},{5,4},{6,5},{7,6},{8,11},{9,8},{10,9... | collective-permute-start | bytes 393224 | tf_op jit(solution)/shard_map/ppermute | solution.py:250
  10.9 0.6 collective-permute-start.2
  11.5 8.3 %collective-permute-start.1 = (f32[256,128]{1,0:T(8,128)S(1)}, f32[256,128]{1,0:T(8,128)S(1)}, u32[]{:S(2)}, u32[]{:S(2)}) collective-permute-start(f32[256,128]{1,0:T(8,128)S(1)} %bitcast.10), channel_id=1, source_target_pairs={{0,124},{1,125},{2,6},{3,7},{4,0},{5,1},{6,10},{7,11},{8,4},{9,5},... | collective-permute-start | bytes 393224 | tf_op jit(solution)/shard_map/ppermute | solution.py:263
  19.8 2.5 %collective-permute-done.1 = f32[256,128]{1,0:T(8,128)S(1)} collective-permute-done((f32[256,128]{1,0:T(8,128)S(1)}, f32[256,128]{1,0:T(8,128)S(1)}, u32[]{:S(2)}, u32[]{:S(2)}) %collective-permute-start.1) | collective-permute-done | bytes 131104 | tf_op jit(solution)/shard_map/ppermute | solution.py:263
  22.3 13.1 %all_to_all.20.slabs_ref = f32[16,2,16,128]{3,2,1,0:T(8,128)S(1)} all-to-all(f32[16,2,16,128]{3,2,1,0:T(8,128)S(1)} %pack.1), channel_id=1, replica_groups=mesh['spin'=2,'y'=4,'z'=8,'x'=4] {'y','x'}, dimensions={0} | all-to-all | bytes 524288 | tf_op jit(solution)/shard_map/all_to_all | solution.py:237
  35.4 4.4 %collective-permute-start.13 = (f32[272,128]{1,0:T(8,128)S(1)}, f32[272,128]{1,0:T(8,128)S(1)}, u32[]{:S(2)}, u32[]{:S(2)}) collective-permute-start(f32[272,128]{1,0:T(8,128)S(1)} %slab.1.refs_0_), channel_id=1, source_target_pairs={{0,16},{4,20},{8,24},{12,28},{16,0},{20,4},{24,8},{28,12},{1,17},{... | collective-permute-start | bytes 417800 | tf_op jit(solution)/shard_map/ppermute | solution.py:250
  39.8 0.7 collective-permute-start.6
  40.5 4.9 %collective-permute-start.5 = (f32[256,128]{1,0:T(8,128)S(1)}, f32[256,128]{1,0:T(8,128)S(1)}, u32[]{:S(2)}, u32[]{:S(2)}) collective-permute-start(f32[256,128]{1,0:T(8,128)S(1)} %collective-permute-done.1), channel_id=1, source_target_pairs={{0,2},{1,3},{2,0},{3,1},{4,6},{5,7},{6,4},{7,5},{8,10},{9,11},{10,... | collective-permute-start | bytes 393224 | tf_op jit(solution)/shard_map/ppermute | solution.py:250
  45.3 3.8 %collective-permute-start.11 = (f32[272,128]{1,0:T(8,128)S(1)}, f32[272,128]{1,0:T(8,128)S(1)}, u32[]{:S(2)}, u32[]{:S(2)}) collective-permute-start(f32[272,128]{1,0:T(8,128)S(1)} %slab.1.refs_0_), channel_id=1, source_target_pairs={{0,12},{4,16},{8,20},{12,24},{16,28},{20,0},{24,4},{28,8},{1,13},{... | collective-permute-start | bytes 417800 | tf_op jit(solution)/shard_map/ppermute | solution.py:250
  49.1 1.0 collective-permute-start.10
  50.1 2.0 %collective-permute-start.9 = (f32[272,128]{1,0:T(8,128)S(1)}, f32[272,128]{1,0:T(8,128)S(1)}, u32[]{:S(2)}, u32[]{:S(2)}) collective-permute-start(f32[272,128]{1,0:T(8,128)S(1)} %slab.1.refs_0_), channel_id=1, source_target_pairs={{0,8},{4,12},{8,16},{12,20},{16,24},{20,28},{24,0},{28,4},{1,9},{5... | collective-permute-start | bytes 417800 | tf_op jit(solution)/shard_map/ppermute | solution.py:250
  52.1 2.3 %collective-permute-start.8 = (f32[272,128]{1,0:T(8,128)S(1)}, f32[272,128]{1,0:T(8,128)S(1)}, u32[]{:S(2)}, u32[]{:S(2)}) collective-permute-start(f32[272,128]{1,0:T(8,128)S(1)} %slab.1.refs_0_), channel_id=1, source_target_pairs={{0,28},{4,0},{8,4},{12,8},{16,12},{20,16},{24,20},{28,24},{1,29},{... | collective-permute-start | bytes 417800 | tf_op jit(solution)/shard_map/ppermute | solution.py:250
  54.3 1.4 %collective-permute-done.12.refs_6_ = f32[272,128]{1,0:T(8,128)S(1)} collective-permute-done((f32[272,128]{1,0:T(8,128)S(1)}, f32[272,128]{1,0:T(8,128)S(1)}, u32[]{:S(2)}, u32[]{:S(2)}) %collective-permute-start.12) | collective-permute-done | bytes 139296 | tf_op jit(solution)/shard_map/ppermute | solution.py:250
  55.8 1.0 collective-permute-start.7
  56.7 2.2 %copy-done.2 = bf16[2,1024,1024]{2,1,0:T(8,128)(2,1)S(1)} copy-done((bf16[2,1024,1024]{2,1,0:T(8,128)(2,1)S(1)}, bf16[2,1024,1024]{2,1,0:T(8,128)(2,1)}, u32[]{:S(2)}) %copy-start.2) | copy-done | bytes 4194328
  58.9 3.9 %pair_fields.1 = f32[256,128]{1,0:T(8,128)} custom-call(s32[1]{0:T(128)} %bitcast.x_ref, f32[256,128]{1,0:T(8,128)S(1)} %bitcast.12, f32[256,128]{1,0:T(8,128)S(1)} %get-tuple-element.17.start_ref, f32[256,128]{1,0:T(8,128)S(1)} %collective-permute-done.2.below, f32[256,128]{1,0:T(8,128)S(1)} %collective-permute-done.3.above, ...), custom_call_target="tpu_custom_call" | custom-call | flops 1073741824 | bytes 8388608 | tf_op jit(solution)/shard_map/pair_fields/pallas_call | solution.py:222
  62.9 6.0 %all-to-all-start.1 = ((f32[16,16,128]{2,1,0:T(8,128)}), f32[16,16,128]{2,1,0:T(8,128)S(1)}, u32[]{:S(2)}, u32[]{:S(2)}) async-start(f32[16,16,128]{2,1,0:T(8,128)} %bitcast.2), calls=%async_computation.1 | async-start | bytes 262144 | tf_op jit(solution)/shard_map/all_to_all | solution.py:237
  68.9 6.7 %all-to-all-done.1.g_ref = f32[16,16,128]{2,1,0:T(8,128)S(1)} async-done(((f32[16,16,128]{2,1,0:T(8,128)}), f32[16,16,128]{2,1,0:T(8,128)S(1)}, u32[]{:S(2)}, u32[]{:S(2)}) %all-to-all-start.1) | async-done | bytes 131104 | tf_op jit(solution)/shard_map/all_to_all | solution.py:237
  75.7 1.1 %correlations.1 = (f32[112,128]{1,0:T(8,128)S(1)}, f32[16,16,128]{2,1,0:T(8,128)S(1)}, bf16[128,2048]{1,0:T(8,128)(2,1)S(1)}, bf16[128,2048]{1,0:T(8,128)(2,1)S(1)}) custom-call(f32[16,16,128]{2,1,0:T(8,128)S(1)} %all-to-all-done.1.g_ref, f32[16,128]{1,0:T(8,128)S(1)} %constant_dynamic-slice_fusion.potential_ref, f32[272,128]{1,0:T(8,128)S(1)} %slab.1.refs_0_, ...), custom_call_target="tpu_custom_call" | custom-call | flops 1073741824 | bytes 8388608 | tf_op jit(solution)/shard_map/correlations/pallas_call | solution.py:222
  76.8 0.1 broadcast_in_dim.2
  76.8 17.6 %all_to_all.21.corr_ref = f32[16,112,128]{2,1,0:T(8,128)S(1)} all-to-all(f32[16,112,128]{2,1,0:T(8,128)S(1)} %broadcast_in_dim.2), channel_id=1, replica_groups=mesh['spin'=2,'y'=4,'z'=8,'x'=4] {'y','x'}, dimensions={0} | all-to-all | bytes 1835008 | tf_op jit(solution)/shard_map/all_to_all | solution.py:237
  94.5 0.6 removal.1
  95.1 10.8 %all_to_all.22 = f32[16,16,128]{2,1,0:T(8,128)S(1)} all-to-all(f32[16,16,128]{2,1,0:T(8,128)S(1)} %removal.1), channel_id=1, replica_groups=mesh['spin'=2,'y'=4,'z'=8,'x'=4] {'y','x'}, dimensions={0} | all-to-all | bytes 262144 | tf_op jit(solution)/shard_map/all_to_all | solution.py:237
  105.8 0.8 multiply_subtract_fusion
  106.7 0.7 copy.7
  (25 shorter events, 0.1 us)
Async XLA Ops:
  0.6 68.3 %copy-start = (f32[32768]{0:T(1024)S(1)}, f32[32768]{0:T(1024)}, u32[]{:S(2)}) copy-start(f32[32768]{0:T(1024)} %param.5) | copy-start | bytes 393220
  0.6 2.2 %copy-start.1 = (bf16[2,1024,1024]{2,1,0:T(8,128)(2,1)S(1)}, bf16[2,1024,1024]{2,1,0:T(8,128)(2,1)}, u32[]{:S(2)}) copy-start(bf16[2,1024,1024]{2,1,0:T(8,128)(2,1)} %constant.22.clone.joined_ref) | copy-start | bytes 12582916
  2.9 0.9 copy-start.3
  3.8 0.8 copy-start.5
  7.1 49.6 %copy-start.4 = (f32[1,1,32768]{2,1,0:T(1,128)S(1)}, f32[1,1,32768]{2,1,0:T(1,128)}, u32[]{:S(2)}) copy-start(f32[1,1,32768]{2,1,0:T(1,128)} %param.4) | copy-start | bytes 393220
  7.1 49.6 %copy-start.6 = (bf16[2,128,128]{2,1,0:T(8,128)(2,1)S(1)}, bf16[2,128,128]{2,1,0:T(8,128)(2,1)}, u32[]{:S(2)}) copy-start(bf16[2,128,128]{2,1,0:T(8,128)(2,1)} %constant.23.clone.lines_ref) | copy-start | bytes 196612
  7.1 12.7 %collective-permute-start = (f32[256,128]{1,0:T(8,128)S(1)}, f32[256,128]{1,0:T(8,128)S(1)}, u32[]{:S(2)}, u32[]{:S(2)}) collective-permute-start(f32[256,128]{1,0:T(8,128)S(1)} %get-tuple-element.15.square_ref), channel_id=1, source_target_pairs={{0,128},{128,0},{1,129},{129,1},{2,130},{130,2},{3,131},{131,3},{4... | collective-permute-start | bytes 393224 | tf_op jit(solution)/shard_map/ppermute | solution.py:250
  7.2 12.6 %collective-permute-start.4 = (f32[256,128]{1,0:T(8,128)S(1)}, f32[256,128]{1,0:T(8,128)S(1)}, u32[]{:S(2)}, u32[]{:S(2)}) collective-permute-start(f32[256,128]{1,0:T(8,128)S(1)} %bitcast.7), channel_id=1, source_target_pairs={{0,2},{1,3},{2,0},{3,1},{4,6},{5,7},{6,4},{7,5},{8,10},{9,11},{10,... | collective-permute-start | bytes 393224 | tf_op jit(solution)/shard_map/ppermute | solution.py:250
  9.5 10.4 %collective-permute-start.3 = (f32[256,128]{1,0:T(8,128)S(1)}, f32[256,128]{1,0:T(8,128)S(1)}, u32[]{:S(2)}, u32[]{:S(2)}) collective-permute-start(f32[256,128]{1,0:T(8,128)S(1)} %bitcast.8), channel_id=1, source_target_pairs={{0,3},{1,0},{2,1},{3,2},{4,7},{5,4},{6,5},{7,6},{8,11},{9,8},{10,9... | collective-permute-start | bytes 393224 | tf_op jit(solution)/shard_map/ppermute | solution.py:250
  10.9 9.0 %collective-permute-start.2 = (f32[256,128]{1,0:T(8,128)S(1)}, f32[256,128]{1,0:T(8,128)S(1)}, u32[]{:S(2)}, u32[]{:S(2)}) collective-permute-start(f32[256,128]{1,0:T(8,128)S(1)} %bitcast.9), channel_id=1, source_target_pairs={{0,1},{1,2},{2,3},{3,0},{4,5},{5,6},{6,7},{7,4},{8,9},{9,10},{10,1... | collective-permute-start | bytes 393224 | tf_op jit(solution)/shard_map/ppermute | solution.py:250
  11.5 10.8 %collective-permute-start.1 = (f32[256,128]{1,0:T(8,128)S(1)}, f32[256,128]{1,0:T(8,128)S(1)}, u32[]{:S(2)}, u32[]{:S(2)}) collective-permute-start(f32[256,128]{1,0:T(8,128)S(1)} %bitcast.10), channel_id=1, source_target_pairs={{0,124},{1,125},{2,6},{3,7},{4,0},{5,1},{6,10},{7,11},{8,4},{9,5},... | collective-permute-start | bytes 393224 | tf_op jit(solution)/shard_map/ppermute | solution.py:263
  35.4 16.7 %collective-permute-start.13 = (f32[272,128]{1,0:T(8,128)S(1)}, f32[272,128]{1,0:T(8,128)S(1)}, u32[]{:S(2)}, u32[]{:S(2)}) collective-permute-start(f32[272,128]{1,0:T(8,128)S(1)} %slab.1.refs_0_), channel_id=1, source_target_pairs={{0,16},{4,20},{8,24},{12,28},{16,0},{20,4},{24,8},{28,12},{1,17},{... | collective-permute-start | bytes 417800 | tf_op jit(solution)/shard_map/ppermute | solution.py:250
  39.8 16.0 %collective-permute-start.12 = (f32[272,128]{1,0:T(8,128)S(1)}, f32[272,128]{1,0:T(8,128)S(1)}, u32[]{:S(2)}, u32[]{:S(2)}) collective-permute-start(f32[272,128]{1,0:T(8,128)S(1)} %slab.1.refs_0_), channel_id=1, source_target_pairs={{0,20},{4,24},{8,28},{12,0},{16,4},{20,8},{24,12},{28,16},{1,21},{... | collective-permute-start | bytes 417800 | tf_op jit(solution)/shard_map/ppermute | solution.py:250
  39.8 9.3 %collective-permute-start.6 = (f32[256,128]{1,0:T(8,128)S(1)}, f32[256,128]{1,0:T(8,128)S(1)}, u32[]{:S(2)}, u32[]{:S(2)}) collective-permute-start(f32[256,128]{1,0:T(8,128)S(1)} %collective-permute-done.1), channel_id=1, source_target_pairs={{0,3},{3,0},{4,7},{7,4},{8,11},{11,8},{12,15},{15,12},{16,19},{19,... | collective-permute-start | bytes 393224 | tf_op jit(solution)/shard_map/ppermute | solution.py:279
  40.5 9.6 %collective-permute-start.5 = (f32[256,128]{1,0:T(8,128)S(1)}, f32[256,128]{1,0:T(8,128)S(1)}, u32[]{:S(2)}, u32[]{:S(2)}) collective-permute-start(f32[256,128]{1,0:T(8,128)S(1)} %collective-permute-done.1), channel_id=1, source_target_pairs={{0,2},{1,3},{2,0},{3,1},{4,6},{5,7},{6,4},{7,5},{8,10},{9,11},{10,... | collective-permute-start | bytes 393224 | tf_op jit(solution)/shard_map/ppermute | solution.py:250
  45.3 30.3 %collective-permute-start.11 = (f32[272,128]{1,0:T(8,128)S(1)}, f32[272,128]{1,0:T(8,128)S(1)}, u32[]{:S(2)}, u32[]{:S(2)}) collective-permute-start(f32[272,128]{1,0:T(8,128)S(1)} %slab.1.refs_0_), channel_id=1, source_target_pairs={{0,12},{4,16},{8,20},{12,24},{16,28},{20,0},{24,4},{28,8},{1,13},{... | collective-permute-start | bytes 417800 | tf_op jit(solution)/shard_map/ppermute | solution.py:250
  49.1 26.5 %collective-permute-start.10 = (f32[272,128]{1,0:T(8,128)S(1)}, f32[272,128]{1,0:T(8,128)S(1)}, u32[]{:S(2)}, u32[]{:S(2)}) collective-permute-start(f32[272,128]{1,0:T(8,128)S(1)} %slab.1.refs_0_), channel_id=1, source_target_pairs={{0,24},{4,28},{8,0},{12,4},{16,8},{20,12},{24,16},{28,20},{1,25},{... | collective-permute-start | bytes 417800 | tf_op jit(solution)/shard_map/ppermute | solution.py:250
  50.1 25.5 %collective-permute-start.9 = (f32[272,128]{1,0:T(8,128)S(1)}, f32[272,128]{1,0:T(8,128)S(1)}, u32[]{:S(2)}, u32[]{:S(2)}) collective-permute-start(f32[272,128]{1,0:T(8,128)S(1)} %slab.1.refs_0_), channel_id=1, source_target_pairs={{0,8},{4,12},{8,16},{12,20},{16,24},{20,28},{24,0},{28,4},{1,9},{5... | collective-permute-start | bytes 417800 | tf_op jit(solution)/shard_map/ppermute | solution.py:250
  52.1 23.6 %collective-permute-start.8 = (f32[272,128]{1,0:T(8,128)S(1)}, f32[272,128]{1,0:T(8,128)S(1)}, u32[]{:S(2)}, u32[]{:S(2)}) collective-permute-start(f32[272,128]{1,0:T(8,128)S(1)} %slab.1.refs_0_), channel_id=1, source_target_pairs={{0,28},{4,0},{8,4},{12,8},{16,12},{20,16},{24,20},{28,24},{1,29},{... | collective-permute-start | bytes 417800 | tf_op jit(solution)/shard_map/ppermute | solution.py:250
  55.8 19.9 %collective-permute-start.7 = (f32[272,128]{1,0:T(8,128)S(1)}, f32[272,128]{1,0:T(8,128)S(1)}, u32[]{:S(2)}, u32[]{:S(2)}) collective-permute-start(f32[272,128]{1,0:T(8,128)S(1)} %slab.1.refs_0_), channel_id=1, source_target_pairs={{0,4},{4,8},{8,12},{12,16},{16,20},{20,24},{24,28},{28,0},{1,5},{5... | collective-permute-start | bytes 417800 | tf_op jit(solution)/shard_map/ppermute | solution.py:250
  56.7 2.2 %copy-start.2 = (bf16[2,1024,1024]{2,1,0:T(8,128)(2,1)S(1)}, bf16[2,1024,1024]{2,1,0:T(8,128)(2,1)}, u32[]{:S(2)}) copy-start(bf16[2,1024,1024]{2,1,0:T(8,128)(2,1)} %constant.22.clone.joined_ref) | copy-start | bytes 12582916
  62.9 12.7 %all-to-all-start.1 = ((f32[16,16,128]{2,1,0:T(8,128)}), f32[16,16,128]{2,1,0:T(8,128)S(1)}, u32[]{:S(2)}, u32[]{:S(2)}) async-start(f32[16,16,128]{2,1,0:T(8,128)} %bitcast.2), calls=%async_computation.1 | async-start | bytes 262144 | tf_op jit(solution)/shard_map/all_to_all | solution.py:237

commit v2 on v1

--- a/solution.py
+++ b/solution.py
@@ -22,10 +22,10 @@
 MIXING = 0.25
 STEP_LENGTH = 0.1
 
-BANDS = ("y", "z", "x")
+BANDS = ("y", "zh", "zl", "x")
 GRID_X = 4
-SLAB = ("y", "x")
-GATHER = ("z",)
+SLAB = ("y", "zl", "x")
+GATHER = ("zh",)
 
 f32 = jnp.float32
 bf16 = jnp.bfloat16
@@ -124,7 +124,7 @@
 ]
 
 
-def own_kernel(o_ref, joined_ref, lines_ref, square_ref, start_ref, joined, lines, sems):
+def own_kernel(o_ref, joined_ref, lines_ref, packed_ref, start_ref, joined, lines, sems):
     copies = table_copies(joined_ref, lines_ref, joined, lines, sems)
     own = to_planes(o_ref)
     fields = jnp.concatenate([own * own, own], axis=0)
@@ -133,16 +133,14 @@
     fields = twice_transformed(fields, factors, joined, lines, copies)
     square, kinetic = fields[:GRID], fields[GRID:]
     start = kinetic - MIXING * square * own
+    parts, rows = packed_ref.shape[0], packed_ref.shape[2]
+    packed_ref[:, 0] = o_ref[...].reshape(parts, rows, LANES)
+    planes = rows // SPLIT
     for j in range(SPLIT):
-        rows = pl.ds(j, GRID, stride=SPLIT)
-        start_ref[rows, :] = start[:, j * LANES : (j + 1) * LANES]
-        square_ref[rows, :] = square[:, j * LANES : (j + 1) * LANES]
-
-
-def pack_kernel(o_ref, square_ref, other_ref, packed_ref):
-    shape = packed_ref.shape[0], packed_ref.shape[2], LANES
-    packed_ref[:, 0] = o_ref[...].reshape(shape)
-    packed_ref[:, 1] = (square_ref[...] + other_ref[...]).reshape(shape)
+        start_ref[pl.ds(j, GRID, stride=SPLIT), :] = start[:, j * LANES : (j + 1) * LANES]
+        piece = square[:, j * LANES : (j + 1) * LANES]
+        for k in range(parts):
+            packed_ref[k, 1, pl.ds(j, planes, stride=SPLIT), :] = piece[k * planes : (k + 1) * planes]
 
 
 def pair_kernel(x_ref, o_ref, start_ref, below, above, second, across, corner, joined_ref, lines_ref, out_ref, joined, lines, sems):
@@ -165,50 +163,51 @@
         out_ref[rows, :] = start_ref[rows, :] - MIXING * total[:, j * LANES : (j + 1) * LANES]
 
 
-def slab_kernel(slabs_ref, out_ref):
+def spread_kernel(slabs_ref, out_ref):
     bands, rows = slabs_ref.shape[0], slabs_ref.shape[2]
-    out_ref[: bands * rows] = slabs_ref[:, 0].reshape(bands * rows, LANES)
-    out_ref[bands * rows :] = jnp.sum(slabs_ref[:, 1], axis=0)
-
-
-def correlate_kernel(g_ref, potential_ref, *refs):
-    pieces, (corr_ref, g_out, oh_ref, ol_ref) = refs[:-4], refs[-4:]
-    bands, rows = g_ref.shape[0], g_ref.shape[1]
     cells = bands * rows
-    count = bands * len(pieces)
-    squares = sum(piece[cells:, :] for piece in pieces)
-    local = potential_ref[...] + HARTREE_WEIGHT * squares
-    g = g_ref[...] + local[None] * pieces[0][:cells].reshape(bands, rows, LANES)
-    g_out[...] = g
-    for k, piece in enumerate(pieces):
+    own = slabs_ref[:, 0].reshape(cells, LANES)
+    square = jnp.sum(slabs_ref[:, 1], axis=0)
+    for k in range(out_ref.shape[0]):
+        out_ref[k, :cells] = own
+        out_ref[k, cells:] = square
+
+
+def overlap_kernel(gathered_ref, gradient_ref, packed_ref, square_ref, oh_ref, ol_ref):
+    groups = gathered_ref.shape[0]
+    rows = square_ref.shape[0]
+    bands = gathered_ref.shape[1] // rows - 1
+    cells = bands * rows
+    square_ref[...] = jnp.sum(gathered_ref[:, cells:, :], axis=0)
+    for k in range(groups):
         for c in range(rows):
-            high, low = split(piece[pl.ds(c, bands, stride=rows), :])
+            high, low = split(gathered_ref[k, pl.ds(c, bands, stride=rows), :])
             oh_ref[k * bands : (k + 1) * bands, c * LANES : (c + 1) * LANES] = high
             ol_ref[k * bands : (k + 1) * bands, c * LANES : (c + 1) * LANES] = low
+    high, low = oh_ref[...], ol_ref[...]
+    mixed = mmt(high, low)
+    overlap = (mmt(high, high) + mixed + mixed.T) * (1.0 / CELLS)
+    packed_ref[:, :rows] = gradient_ref[...].reshape(bands, rows, LANES)
+    packed_ref[:, rows:] = overlap.reshape(bands, overlap.shape[0] // bands, LANES)
+
+
+def correlate_kernel(slabs_ref, own_ref, potential_ref, square_ref, other_ref, oh_ref, ol_ref, corr_ref, g_out):
+    bands, rows = g_out.shape[0], g_out.shape[1]
+    local = potential_ref[...] + HARTREE_WEIGHT * (square_ref[...] + other_ref[...])
+    g = slabs_ref[:, :rows] + local[None] * own_ref[:, 0]
+    g_out[...] = g
     wide = jnp.concatenate([g[:, c, :] for c in range(rows)], axis=1)
-    g_high, g_low = split(wide)
-    high, low = oh_ref[...], ol_ref[...]
-    left_high = jnp.concatenate([g_high, high], axis=0)
-    left_low = jnp.concatenate([g_low, low], axis=0)
-    total = mmt(left_high, high) + mmt(left_low, high) + mmt(left_high, low)
-    total = total * (1.0 / CELLS)
-    half = count // 2
-    quarter = half // 2
-    kept = bands + half
-    corner = total[kept:, half:]
-    corr_ref[:kept] = total[:kept]
-    corr_ref[kept:] = jnp.concatenate([corner[:quarter], corner[quarter:]], axis=1)
+    first = product(wide, oh_ref[...], ol_ref[...], mmt) * (1.0 / CELLS)
+    overlap = jnp.sum(slabs_ref[:, rows:], axis=0)
+    for k in range(bands):
+        corr_ref[k, :bands] = first
+        corr_ref[k, bands:] = overlap
 
 
 def remove_kernel(corr_ref, g_ref, oh_ref, ol_ref, out_ref):
     bands, rows = g_ref.shape[0], g_ref.shape[1]
-    corr = jnp.sum(corr_ref[...], axis=0)
-    half = corr.shape[1] // 2
-    kept = bands + half
-    first, upper, corner = corr[:bands], corr[bands:kept], corr[kept:]
-    lower = jnp.concatenate([corner[:, :half], corner[:, half:]], axis=0)
-    lower = jnp.concatenate([upper[:, half:].T, lower], axis=1)
-    overlap = jnp.concatenate([upper, lower], axis=0)
+    first = jnp.sum(corr_ref[:, :bands], axis=0)
+    overlap = corr_ref[:, bands:].reshape(LANES, LANES)
     s_high, s_low = split(overlap)
     weights = 2.0 * first - product(first, s_high, s_low, mm)
     taken = product(weights, oh_ref[...], ol_ref[...], mm)
@@ -216,7 +215,13 @@
         out_ref[:, c, :] = g_ref[:, c, :] - taken[:, c * LANES : (c + 1) * LANES]
 
 
-def call(kernel, outs, args, name, tables=(), flops=1 << 30, nbytes=1 << 23):
+def update_kernel(o_ref, residual_ref, updated_ref, out_ref):
+    residual = residual_ref[...]
+    out_ref[...] = residual
+    updated_ref[...] = o_ref[...] - STEP_LENGTH * residual
+
+
+def call(kernel, outs, args, name, tables=(), limit=40, flops=1 << 30, nbytes=1 << 23):
     single = not isinstance(outs, list)
     shapes = [outs] if single else outs
     result = pl.pallas_call(
@@ -225,7 +230,7 @@
         in_specs=[pl.BlockSpec(memory_space=pltpu.SMEM if a.dtype == jnp.int32 else pltpu.VMEM) for a in args]
         + [pl.BlockSpec(memory_space=pltpu.HBM)] * len(tables),
         out_specs=[pl.BlockSpec(memory_space=pltpu.VMEM)] * len(shapes),
-        compiler_params=pltpu.CompilerParams(vmem_limit_bytes=40 << 20),
+        compiler_params=pltpu.CompilerParams(vmem_limit_bytes=limit << 20),
         cost_estimate=pl.CostEstimate(flops=flops, bytes_accessed=nbytes, transcendentals=0),
         scratch_shapes=TABLE_SCRATCH if tables else [],
         name=name,
@@ -258,28 +263,29 @@
 
     own = orbitals.reshape(ROWS, LANES)
     below, above, second = (shifted(own, ("x",), by) for by in (1, -1, 2))
-    rings = size(("y", "z"))
+    rings = size(BANDS[:-1])
     toward = [-1, -1, 1, 1]
     edge = lax.ppermute(
         own,
         BANDS,
         [(g * GRID_X + x, (g + toward[x]) % rings * GRID_X + x) for g in range(rings) for x in range(GRID_X)],
     )
-    square, start = call(
+    packed, start = call(
         own_kernel,
-        [((ROWS, LANES), f32), ((ROWS, LANES), f32)],
+        [((parts, 2, rows, LANES), f32), ((ROWS, LANES), f32)],
         [own],
         "own_fields",
         tables,
-    )
-    other = shifted(square, ("spin",), 1)
-    packed = call(pack_kernel, ((parts, 2, rows, LANES), f32), [own, square, other], "pack")
-    packed, start, edge, below, above, second = lax.optimization_barrier((packed, start, edge, below, above, second))
+        60,
+    )
+    packed, edge, below, above, second = lax.optimization_barrier((packed, edge, below, above, second))
+    slabs = exchange(packed, SLAB)
+    spread = call(spread_kernel, ((groups, (parts + 1) * rows, LANES), f32), [slabs], "spread")
+    gathered = exchange(spread, GATHER)
+
+    edge, spread = lax.optimization_barrier((edge, spread))
     across = shifted(edge, ("x",), 2)
     corner = lax.ppermute(edge, "x", [(0, GRID_X - 1), (GRID_X - 1, 0)])
-    slabs = exchange(packed, SLAB)
-    slab = call(slab_kernel, (((parts + 1) * rows, LANES), f32), [slabs], "slab")
-    pieces = [slab] + [shifted(slab, GATHER, by) for by in (1, -1, 2, -2, 3, -3, 4)]
     gradient = call(
         pair_kernel,
         ((ROWS, LANES), f32),
@@ -287,35 +293,46 @@
         "pair_fields",
         tables,
     )
-    gradient, slab = lax.optimization_barrier((gradient, slab))
-    slab_gradient = exchange(gradient.reshape(parts, rows, LANES), SLAB)
-    here = lax.axis_index(SLAB)
-    slab_potential = lax.dynamic_slice_in_dim(potential.reshape(ROWS, LANES), here * rows, rows, 0)
+
     bands = parts * groups
-    corr, slab_gradient, o_high, o_low = call(
-        correlate_kernel,
+    share = bands // parts
+    packed, square, o_high, o_low = call(
+        overlap_kernel,
         [
-            ((parts + 3 * bands // 4, LANES), f32),
-            ((parts, rows, LANES), f32),
+            ((parts, rows + share, LANES), f32),
+            ((rows, LANES), f32),
             ((bands, rows * LANES), bf16),
             ((bands, rows * LANES), bf16),
         ],
-        [slab_gradient, slab_potential, *pieces],
+        [gathered, gradient],
+        "overlaps",
+    )
+    other = shifted(square, ("spin",), 1)
+    slab_gradient = exchange(packed, SLAB)
+    here = lax.axis_index(SLAB)
+    slab_potential = lax.dynamic_slice_in_dim(potential.reshape(ROWS, LANES), here * rows, rows, 0)
+    corr, slab_gradient = call(
+        correlate_kernel,
+        [((parts, parts + share, LANES), f32), ((parts, rows, LANES), f32)],
+        [slab_gradient, slabs, slab_potential, square, other, o_high, o_low],
         "correlations",
     )
-    spread = gather(corr, SLAB)
+    corr = exchange(corr, SLAB)
     slab_residual = call(
         remove_kernel,
         ((parts, rows, LANES), f32),
-        [spread, slab_gradient, o_high, o_low],
+        [corr, slab_gradient, o_high, o_low],
         "removal",
     )
-    residual = exchange(slab_residual, SLAB).reshape(1, 1, CELLS)
-    return orbitals - STEP_LENGTH * residual, residual
+    residual = exchange(slab_residual, SLAB).reshape(ROWS, LANES)
+    updated, residual = call(
+        update_kernel, [((ROWS, LANES), f32), ((ROWS, LANES), f32)], [own, residual], "update"
+    )
+    return updated.reshape(1, 1, CELLS), residual.reshape(1, 1, CELLS)
 
 
 def solution(mesh):
-    fine = Mesh(mesh.devices.reshape(2, 4, 8, 4), ("spin",) + BANDS)
+    fine = Mesh(mesh.devices.reshape(2, 4, 4, 2, 4), ("spin",) + BANDS)
     spec = P("spin", BANDS, None)
     return jax.shard_map(
         per_device, mesh=fine, in_specs=(spec, P()), out_specs=(spec, spec), check_vma=False

time: 108 us -> 96.2 us (0.89)
  starting transfers between devices: 38.6 us -> 24.4 us
  local copies, waits for them, and re-layouts: 6.9 us -> 2.22 us
  Pallas kernels: 8.16 us -> 12.4 us
  waiting for transfers between devices: 10.6 us -> 14.2 us
    ppermute x12 -> x5, starting transfers between devices: 23.6 us -> 3.55 us  [shifted(): return lax.ppermute(x, axes, [(i, (i + by) % peers) for i in range(peers)])]
    all_to_all x1 -> x2, starting transfers between devices: 6.03 us -> 11.8 us  [exchange(): return lax.all_to_all(x, axes, 0, 0, tiled=True)]
    ppermute x12 -> x5, waiting for transfers between devices: 1.44 us -> 6.49 us  [shifted(): return lax.ppermute(x, axes, [(i, (i + by) % peers) for i in range(peers)])]
    unnamed x15 -> x10, local copies, waits for them, and re-layouts: 6.83 us -> 2.21 us
    pallas_call x6 -> x7, Pallas kernels: 8.16 us -> 12.4 us  [call(): pl.pallas_call(kernel, out_shape=[jax.ShapeDtypeStruct(s, t) for s, t in...]
    ppermute x1, waiting for transfers between devices: 2.46 us -> 0.01 us  [per_device(): lax.ppermute(own, BANDS, [(g * GRID_X + x, (g + toward[x]) % rings * GRID...]
    all_to_all x1 -> x2, waiting for transfers between devices: 6.69 us -> 7.7 us  [exchange(): return lax.all_to_all(x, axes, 0, 0, tiled=True)]
  transfers between devices with their start and end apart: 15 -> 9, of which waited for: 3 -> 5; matrix products, arithmetic and copies ran while one was open for 0% -> 0% of each run, Pallas kernels for 4% -> 9%
where the time goes in v2:
time: 96.2 us; the launch traced here: 95.3 us
  blocking collectives  41.3 us (43%)
  starting transfers between devices  24.4 us (25%)
  waiting for transfers between devices  14.2 us (15%)
  Pallas kernels  12.4 us (13%)
  local copies, waits for them, and re-layouts  2.22 us (2%)
    all_to_all x3, blocking collectives, exchange(): return lax.all_to_all(x, axes, 0, 0, tiled=True)  41.3 us
    pallas_call x7, Pallas kernels, call(): pl.pallas_call(kernel, out_shape=[jax.ShapeDtypeStruct(s, t) for s, t in...  12.4 us
    all_to_all x2, starting transfers between devices, exchange(): return lax.all_to_all(x, axes, 0, 0, tiled=True)  11.8 us
    ppermute x1, starting transfers between devices, per_device(): lax.ppermute(own, BANDS, [(g * GRID_X + x, (g + toward[x]) % rings * GRID...  8.38 us
    all_to_all x2, waiting for transfers between devices, exchange(): return lax.all_to_all(x, axes, 0, 0, tiled=True)  7.7 us
    ppermute x5, waiting for transfers between devices, shifted(): return lax.ppermute(x, axes, [(i, (i + by) % peers) for i in range(peers)])  6.49 us
    ppermute x5, starting transfers between devices, shifted(): return lax.ppermute(x, axes, [(i, (i + by) % peers) for i in range(peers)])  3.55 us
    unnamed x10, local copies, waits for them, and re-layouts  2.21 us
  transfers between devices with their start and end apart: 9, of which 5 were waited for; matrix products, arithmetic and copies ran while one was open for 0% of the time, Pallas kernels for 9%

profile of v2, /device:TPU:2, one launch (start us, length us, event | category | flops | bytes accessed | tf_op | source)
XLA Modules:
  0.0 95.3 jit_solution(6737145584513702841)
XLA Ops:
  0.6 0.0 copy-start
  0.7 0.0 copy-start.3
  0.7 8.4 %collective-permute-start = (f32[256,128]{1,0:T(8,128)}, f32[256,128]{1,0:T(8,128)S(1)}, u32[]{:S(2)}, u32[]{:S(2)}) collective-permute-start(f32[256,128]{1,0:T(8,128)} %bitcast.7), channel_id=1, source_target_pairs={{0,124},{1,125},{2,6},{3,7},{4,0},{5,1},{6,10},{7,11},{8,4},{9,5},... | collective-permute-start | bytes 393224 | tf_op jit(solution)/shard_map/ppermute | solution.py:268
  9.1 0.0 collective-permute-start.1
  9.1 2.0 %collective-permute-start.2 = (f32[256,128]{1,0:T(8,128)}, f32[256,128]{1,0:T(8,128)S(1)}, u32[]{:S(2)}, u32[]{:S(2)}) collective-permute-start(f32[256,128]{1,0:T(8,128)} %bitcast.9), channel_id=1, source_target_pairs={{0,3},{1,0},{2,1},{3,2},{4,7},{5,4},{6,5},{7,6},{8,11},{9,8},{10,9... | collective-permute-start | bytes 393224 | tf_op jit(solution)/shard_map/ppermute | solution.py:255
  11.1 0.6 collective-permute-start.3
  11.7 5.6 %own_fields.1 = (f32[32,2,8,128]{3,2,1,0:T(8,128)}, f32[256,128]{1,0:T(8,128)}) custom-call(f32[256,128]{1,0:T(8,128)} %bitcast.11, bf16[2,1024,1024]{2,1,0:T(8,128)(2,1)} %constant.25.clone.joined_ref, bf16[2,128,128]{2,1,0:T(8,128)(2,1)} %constant.26.clone.lines_ref), custom_call_target="tpu_custom_call" | custom-call | flops 1073741824 | bytes 8388608 | tf_op jit(solution)/shard_map/own_fields/pallas_call | solution.py:227
  17.3 0.0 copy-start.4
  17.3 0.0 collective-permute-done
  17.3 0.0 collective-permute-done.1.below
  17.3 0.4 collective-permute-done.3.second
  17.8 14.1 %all_to_all.25.slabs_ref.own_ref = f32[32,2,8,128]{3,2,1,0:T(8,128)S(1)} all-to-all(f32[32,2,8,128]{3,2,1,0:T(8,128)} %get-tuple-element.19), channel_id=1, replica_groups=mesh['spin'=2,'y'=4,'zh'=4,'zl'=2,'x'=4] {'y','zl','x'}, dimensions={0} | all-to-all | bytes 524288 | tf_op jit(solution)/shard_map/all_to_all | solution.py:242
  31.9 0.9 spread.1
  32.7 4.1 %all-to-all-start.1 = ((f32[4,264,128]{2,1,0:T(8,128)}), f32[4,264,128]{2,1,0:T(8,128)S(1)}, u32[]{:S(2)}, u32[]{:S(2)}) async-start(f32[4,264,128]{2,1,0:T(8,128)} %spread.1), calls=%async_computation.1 | async-start | bytes 1081344 | tf_op jit(solution)/shard_map/all_to_all | solution.py:242
  36.8 0.9 collective-permute-start.4
  37.6 0.7 collective-permute-start.5
  38.3 4.9 %collective-permute-done.4.across = f32[256,128]{1,0:T(8,128)S(1)} collective-permute-done((f32[256,128]{1,0:T(8,128)S(1)}, f32[256,128]{1,0:T(8,128)S(1)}, u32[]{:S(2)}, u32[]{:S(2)}) %collective-permute-start.4) | collective-permute-done | bytes 131104 | tf_op jit(solution)/shard_map/ppermute | solution.py:255
  43.2 0.0 collective-permute-done.5.corner
  43.3 0.0 copy-start.1
  43.3 2.2 %copy-done.1 = bf16[2,1024,1024]{2,1,0:T(8,128)(2,1)S(1)} copy-done((bf16[2,1024,1024]{2,1,0:T(8,128)(2,1)S(1)}, bf16[2,1024,1024]{2,1,0:T(8,128)(2,1)}, u32[]{:S(2)}) %copy-start.1) | copy-done | bytes 4194328
  45.5 3.3 %pair_fields.1.gradient_ref = f32[256,128]{1,0:T(8,128)S(1)} custom-call(s32[1]{0:T(128)} %bitcast.1.x_ref, f32[256,128]{1,0:T(8,128)S(1)} %bitcast.12, f32[256,128]{1,0:T(8,128)S(1)} %copy-done.4, f32[256,128]{1,0:T(8,128)S(1)} %collective-permute-done.1.below, f32[256,128]{1,0:T(8,128)S(1)} %collective-permute-done.2.above, ...), custom_call_target="tpu_custom_call" | custom-call | flops 1073741824 | bytes 8388608 | tf_op jit(solution)/shard_map/pair_fields/pallas_call | solution.py:227
  48.8 0.8 all-to-all-done.1.gathered_ref
  49.5 1.1 %overlaps.1 = (f32[32,12,128]{2,1,0:T(8,128)}, f32[8,128]{1,0:T(8,128)S(1)}, bf16[128,1024]{1,0:T(8,128)(2,1)S(1)}, bf16[128,1024]{1,0:T(8,128)(2,1)S(1)}) custom-call(f32[4,264,128]{2,1,0:T(8,128)S(1)} %all-to-all-done.1.gathered_ref, f32[256,128]{1,0:T(8,128)S(1)} %pair_fields.1.gradient_ref), custom_call_target="tpu_custom_call" | custom-call | flops 1073741824 | bytes 8388608 | tf_op jit(solution)/shard_map/overlaps/pallas_call | solution.py:227
  50.7 7.7 %all-to-all-start.2 = ((f32[32,12,128]{2,1,0:T(8,128)}), f32[32,12,128]{2,1,0:T(8,128)S(1)}, u32[]{:S(2)}, u32[]{:S(2)}) async-start(f32[32,12,128]{2,1,0:T(8,128)} %get-tuple-element.26), calls=%async_computation.2 | async-start | bytes 524288 | tf_op jit(solution)/shard_map/all_to_all | solution.py:242
  58.4 0.1 collective-permute-start.6
  58.5 1.1 %collective-permute-done.6.other_ref = f32[8,128]{1,0:T(8,128)S(1)} collective-permute-done((f32[8,128]{1,0:T(8,128)S(1)}, f32[8,128]{1,0:T(8,128)S(1)}, u32[]{:S(2)}, u32[]{:S(2)}) %collective-permute-start.6) | collective-permute-done | bytes 4128 | tf_op jit(solution)/shard_map/ppermute | solution.py:255
  59.7 6.9 %all-to-all-done.2.slabs_ref = f32[32,12,128]{2,1,0:T(8,128)S(1)} async-done(((f32[32,12,128]{2,1,0:T(8,128)}), f32[32,12,128]{2,1,0:T(8,128)S(1)}, u32[]{:S(2)}, u32[]{:S(2)}) %all-to-all-start.2) | async-done | bytes 196640 | tf_op jit(solution)/shard_map/all_to_all | solution.py:242
  66.6 0.3 correlations.1
  66.9 14.8 %all_to_all.26.corr_ref = f32[32,36,128]{2,1,0:T(8,128)S(1)} all-to-all(f32[32,36,128]{2,1,0:T(8,128)S(1)} %get-tuple-element.30), channel_id=1, replica_groups=mesh['spin'=2,'y'=4,'zh'=4,'zl'=2,'x'=4] {'y','zl','x'}, dimensions={0} | all-to-all | bytes 1179648 | tf_op jit(solution)/shard_map/all_to_all | solution.py:242
  81.7 0.4 removal.1
  82.1 12.5 %all_to_all.27 = f32[32,8,128]{2,1,0:T(8,128)S(1)} all-to-all(f32[32,8,128]{2,1,0:T(8,128)S(1)} %removal.1), channel_id=1, replica_groups=mesh['spin'=2,'y'=4,'zh'=4,'zl'=2,'x'=4] {'y','zl','x'}, dimensions={0} | all-to-all | bytes 262144 | tf_op jit(solution)/shard_map/all_to_all | solution.py:242
  94.6 0.7 update.1
  (7 shorter events, 0.0 us)
Async XLA Ops:
  0.6 57.9 %copy-start = (f32[32768]{0:T(1024)S(1)}, f32[32768]{0:T(1024)}, u32[]{:S(2)}) copy-start(f32[32768]{0:T(1024)} %param.5) | copy-start | bytes 393220
  0.6 42.6 %copy-start.2 = (f32[1,1,32768]{2,1,0:T(1,128)S(1)}, f32[1,1,32768]{2,1,0:T(1,128)}, u32[]{:S(2)}) copy-start(f32[1,1,32768]{2,1,0:T(1,128)} %param.4) | copy-start | bytes 393220
  0.7 42.6 %copy-start.3 = (bf16[2,128,128]{2,1,0:T(8,128)(2,1)S(1)}, bf16[2,128,128]{2,1,0:T(8,128)(2,1)}, u32[]{:S(2)}) copy-start(bf16[2,128,128]{2,1,0:T(8,128)(2,1)} %constant.26.clone.lines_ref) | copy-start | bytes 196612
  0.7 16.7 %collective-permute-start = (f32[256,128]{1,0:T(8,128)}, f32[256,128]{1,0:T(8,128)S(1)}, u32[]{:S(2)}, u32[]{:S(2)}) collective-permute-start(f32[256,128]{1,0:T(8,128)} %bitcast.7), channel_id=1, source_target_pairs={{0,124},{1,125},{2,6},{3,7},{4,0},{5,1},{6,10},{7,11},{8,4},{9,5},... | collective-permute-start | bytes 393224 | tf_op jit(solution)/shard_map/ppermute | solution.py:268
  9.1 8.3 %collective-permute-start.1 = (f32[256,128]{1,0:T(8,128)}, f32[256,128]{1,0:T(8,128)S(1)}, u32[]{:S(2)}, u32[]{:S(2)}) collective-permute-start(f32[256,128]{1,0:T(8,128)} %bitcast.8), channel_id=1, source_target_pairs={{0,1},{1,2},{2,3},{3,0},{4,5},{5,6},{6,7},{7,4},{8,9},{9,10},{10,1... | collective-permute-start | bytes 393224 | tf_op jit(solution)/shard_map/ppermute | solution.py:255
  9.1 8.3 %collective-permute-start.2 = (f32[256,128]{1,0:T(8,128)}, f32[256,128]{1,0:T(8,128)S(1)}, u32[]{:S(2)}, u32[]{:S(2)}) collective-permute-start(f32[256,128]{1,0:T(8,128)} %bitcast.9), channel_id=1, source_target_pairs={{0,3},{1,0},{2,1},{3,2},{4,7},{5,4},{6,5},{7,6},{8,11},{9,8},{10,9... | collective-permute-start | bytes 393224 | tf_op jit(solution)/shard_map/ppermute | solution.py:255
  11.1 6.7 %collective-permute-start.3 = (f32[256,128]{1,0:T(8,128)}, f32[256,128]{1,0:T(8,128)S(1)}, u32[]{:S(2)}, u32[]{:S(2)}) collective-permute-start(f32[256,128]{1,0:T(8,128)} %bitcast.10), channel_id=1, source_target_pairs={{0,2},{1,3},{2,0},{3,1},{4,6},{5,7},{6,4},{7,5},{8,10},{9,11},{10,... | collective-permute-start | bytes 393224 | tf_op jit(solution)/shard_map/ppermute | solution.py:255
  17.3 26.0 %copy-start.4 = (f32[256,128]{1,0:T(8,128)S(1)}, f32[256,128]{1,0:T(8,128)}, u32[]{:S(2)}) copy-start(f32[256,128]{1,0:T(8,128)} %get-tuple-element.20.start_ref) | copy-start | bytes 393220
  32.7 16.8 %all-to-all-start.1 = ((f32[4,264,128]{2,1,0:T(8,128)}), f32[4,264,128]{2,1,0:T(8,128)S(1)}, u32[]{:S(2)}, u32[]{:S(2)}) async-start(f32[4,264,128]{2,1,0:T(8,128)} %spread.1), calls=%async_computation.1 | async-start | bytes 1081344 | tf_op jit(solution)/shard_map/all_to_all | solution.py:242
  36.8 6.5 %collective-permute-start.4 = (f32[256,128]{1,0:T(8,128)S(1)}, f32[256,128]{1,0:T(8,128)S(1)}, u32[]{:S(2)}, u32[]{:S(2)}) collective-permute-start(f32[256,128]{1,0:T(8,128)S(1)} %collective-permute-done), channel_id=1, source_target_pairs={{0,2},{1,3},{2,0},{3,1},{4,6},{5,7},{6,4},{7,5},{8,10},{9,11},{10,... | collective-permute-start | bytes 393224 | tf_op jit(solution)/shard_map/ppermute | solution.py:255
  37.6 5.6 %collective-permute-start.5 = (f32[256,128]{1,0:T(8,128)S(1)}, f32[256,128]{1,0:T(8,128)S(1)}, u32[]{:S(2)}, u32[]{:S(2)}) collective-permute-start(f32[256,128]{1,0:T(8,128)S(1)} %collective-permute-done), channel_id=1, source_target_pairs={{0,3},{3,0},{4,7},{7,4},{8,11},{11,8},{12,15},{15,12},{16,19},{19,... | collective-permute-start | bytes 393224 | tf_op jit(solution)/shard_map/ppermute | solution.py:288
  43.3 2.2 %copy-start.1 = (bf16[2,1024,1024]{2,1,0:T(8,128)(2,1)S(1)}, bf16[2,1024,1024]{2,1,0:T(8,128)(2,1)}, u32[]{:S(2)}) copy-start(bf16[2,1024,1024]{2,1,0:T(8,128)(2,1)} %constant.25.clone.joined_ref) | copy-start | bytes 12582916
  50.7 15.9 %all-to-all-start.2 = ((f32[32,12,128]{2,1,0:T(8,128)}), f32[32,12,128]{2,1,0:T(8,128)S(1)}, u32[]{:S(2)}, u32[]{:S(2)}) async-start(f32[32,12,128]{2,1,0:T(8,128)} %get-tuple-element.26), calls=%async_computation.2 | async-start | bytes 524288 | tf_op jit(solution)/shard_map/all_to_all | solution.py:242
  58.4 1.3 %collective-permute-start.6 = (f32[8,128]{1,0:T(8,128)S(1)}, f32[8,128]{1,0:T(8,128)S(1)}, u32[]{:S(2)}, u32[]{:S(2)}) collective-permute-start(f32[8,128]{1,0:T(8,128)S(1)} %get-tuple-element.27.square_ref), channel_id=1, source_target_pairs={{0,128},{128,0},{1,129},{129,1},{2,130},{130,2},{3,131},{131,3},{4... | collective-permute-start | bytes 12296 | tf_op jit(solution)/shard_map/ppermute | solution.py:255

commit v3 on v2

--- a/solution.py
+++ b/solution.py
@@ -24,7 +24,7 @@
 
 BANDS = ("y", "zh", "zl", "x")
 GRID_X = 4
-SLAB = ("y", "zl", "x")
+SLAB = ("zl", "x", "y")
 GATHER = ("zh",)
 
 f32 = jnp.float32
@@ -285,7 +285,7 @@
 
     edge, spread = lax.optimization_barrier((edge, spread))
     across = shifted(edge, ("x",), 2)
-    corner = lax.ppermute(edge, "x", [(0, GRID_X - 1), (GRID_X - 1, 0)])
+    corner = lax.ppermute(edge, "x", [(i, GRID_X - 1 - i) for i in range(GRID_X)])
     gradient = call(
         pair_kernel,
         ((ROWS, LANES), f32),

time: 96.2 us -> 94 us (0.977)
  waiting for transfers between devices: 14.2 us -> 13 us
    all_to_all x2, starting transfers between devices: 11.8 us -> 9.77 us  [exchange(): return lax.all_to_all(x, axes, 0, 0, tiled=True)]
    ppermute x5, waiting for transfers between devices: 6.49 us -> 5.14 us  [shifted(): return lax.ppermute(x, axes, [(i, (i + by) % peers) for i in range(peers)])]
    ppermute x1, waiting for transfers between devices: 0.01 us -> 1.3 us  [per_device(): lax.ppermute(edge, 'x', [(i, GRID_X - 1 - i) for i in range(GRID_X)])]
    all_to_all x2, waiting for transfers between devices: 7.7 us -> 6.6 us  [exchange(): return lax.all_to_all(x, axes, 0, 0, tiled=True)]
  transfers between devices with their start and end apart: 9 -> 9, of which waited for: 5 -> 5; matrix products, arithmetic and copies ran while one was open for 0% -> 0% of each run, Pallas kernels for 9% -> 10%
where the time goes in v3:
time: 94 us; the launch traced here: 93.1 us
  blocking collectives  40.9 us (44%)
  starting transfers between devices  23.8 us (25%)
  waiting for transfers between devices  13 us (14%)
  Pallas kernels  12.3 us (13%)
  local copies, waits for them, and re-layouts  2.22 us (2%)
    all_to_all x3, blocking collectives, exchange(): return lax.all_to_all(x, axes, 0, 0, tiled=True)  40.9 us
    pallas_call x7, Pallas kernels, call(): pl.pallas_call(kernel, out_shape=[jax.ShapeDtypeStruct(s, t) for s, t in...  12.3 us
    all_to_all x2, starting transfers between devices, exchange(): return lax.all_to_all(x, axes, 0, 0, tiled=True)  9.77 us
    ppermute x1, starting transfers between devices, per_device(): lax.ppermute(own, BANDS, [(g * GRID_X + x, (g + toward[x]) % rings * GRID...  8.38 us
    all_to_all x2, waiting for transfers between devices, exchange(): return lax.all_to_all(x, axes, 0, 0, tiled=True)  6.6 us
    ppermute x5, waiting for transfers between devices, shifted(): return lax.ppermute(x, axes, [(i, (i + by) % peers) for i in range(peers)])  5.14 us
    ppermute x5, starting transfers between devices, shifted(): return lax.ppermute(x, axes, [(i, (i + by) % peers) for i in range(peers)])  4.37 us
    unnamed x10, local copies, waits for them, and re-layouts  2.21 us
  transfers between devices with their start and end apart: 9, of which 5 were waited for; matrix products, arithmetic and copies ran while one was open for 0% of the time, Pallas kernels for 10%

profile of v3, /device:TPU:2, one launch (start us, length us, event | category | flops | bytes accessed | tf_op | source)
XLA Modules:
  0.0 93.1 jit_solution(11568461696706226705)
XLA Ops:
  0.6 0.0 copy-start
  0.7 0.0 copy-start.3
  0.7 8.4 %collective-permute-start = (f32[256,128]{1,0:T(8,128)}, f32[256,128]{1,0:T(8,128)S(1)}, u32[]{:S(2)}, u32[]{:S(2)}) collective-permute-start(f32[256,128]{1,0:T(8,128)} %bitcast.7), channel_id=1, source_target_pairs={{0,124},{1,125},{2,6},{3,7},{4,0},{5,1},{6,10},{7,11},{8,4},{9,5},... | collective-permute-start | bytes 393224 | tf_op jit(solution)/shard_map/ppermute | solution.py:268
  9.1 0.0 collective-permute-start.1
  9.1 2.0 %collective-permute-start.2 = (f32[256,128]{1,0:T(8,128)}, f32[256,128]{1,0:T(8,128)S(1)}, u32[]{:S(2)}, u32[]{:S(2)}) collective-permute-start(f32[256,128]{1,0:T(8,128)} %bitcast.9), channel_id=1, source_target_pairs={{0,3},{1,0},{2,1},{3,2},{4,7},{5,4},{6,5},{7,6},{8,11},{9,8},{10,9... | collective-permute-start | bytes 393224 | tf_op jit(solution)/shard_map/ppermute | solution.py:255
  11.1 0.6 collective-permute-start.3
  11.7 5.6 %own_fields.1 = (f32[32,2,8,128]{3,2,1,0:T(8,128)}, f32[256,128]{1,0:T(8,128)}) custom-call(f32[256,128]{1,0:T(8,128)} %bitcast.11, bf16[2,1024,1024]{2,1,0:T(8,128)(2,1)} %constant.27.clone.joined_ref, bf16[2,128,128]{2,1,0:T(8,128)(2,1)} %constant.28.clone.lines_ref), custom_call_target="tpu_custom_call" | custom-call | flops 1073741824 | bytes 8388608 | tf_op jit(solution)/shard_map/own_fields/pallas_call | solution.py:227
  17.3 0.0 copy-start.4
  17.3 0.0 collective-permute-done
  17.3 0.0 collective-permute-done.1.below
  17.3 0.0 collective-permute-done.2.above
  17.3 0.4 collective-permute-done.3.second
  17.8 13.8 %all_to_all.25.slabs_ref.own_ref = f32[32,2,8,128]{3,2,1,0:T(8,128)S(1)} all-to-all(f32[32,2,8,128]{3,2,1,0:T(8,128)} %get-tuple-element.19), channel_id=1, replica_groups=mesh['spin'=2,'y'=4,'zh'=4,'zl'=2,'x'=4] {'zl','x','y'}, dimensions={0} | all-to-all | bytes 524288 | tf_op jit(solution)/shard_map/all_to_all | solution.py:242
  31.5 0.9 spread.1
  32.4 4.1 %all-to-all-start.1 = ((f32[4,264,128]{2,1,0:T(8,128)}), f32[4,264,128]{2,1,0:T(8,128)S(1)}, u32[]{:S(2)}, u32[]{:S(2)}) async-start(f32[4,264,128]{2,1,0:T(8,128)} %spread.1), calls=%async_computation.1 | async-start | bytes 1081344 | tf_op jit(solution)/shard_map/all_to_all | solution.py:242
  36.4 1.7 %collective-permute-start.4 = (f32[256,128]{1,0:T(8,128)S(1)}, f32[256,128]{1,0:T(8,128)S(1)}, u32[]{:S(2)}, u32[]{:S(2)}) collective-permute-start(f32[256,128]{1,0:T(8,128)S(1)} %collective-permute-done), channel_id=1, source_target_pairs={{0,2},{1,3},{2,0},{3,1},{4,6},{5,7},{6,4},{7,5},{8,10},{9,11},{10,... | collective-permute-start | bytes 393224 | tf_op jit(solution)/shard_map/ppermute | solution.py:255
  38.1 1.3 %collective-permute-start.5 = (f32[256,128]{1,0:T(8,128)S(1)}, f32[256,128]{1,0:T(8,128)S(1)}, u32[]{:S(2)}, u32[]{:S(2)}) collective-permute-start(f32[256,128]{1,0:T(8,128)S(1)} %collective-permute-done), channel_id=1, source_target_pairs={{0,3},{1,2},{2,1},{3,0},{4,7},{5,6},{6,5},{7,4},{8,11},{9,10},{10,... | collective-permute-start | bytes 393224 | tf_op jit(solution)/shard_map/ppermute | solution.py:288
  39.4 3.6 %collective-permute-done.4.across = f32[256,128]{1,0:T(8,128)S(1)} collective-permute-done((f32[256,128]{1,0:T(8,128)S(1)}, f32[256,128]{1,0:T(8,128)S(1)}, u32[]{:S(2)}, u32[]{:S(2)}) %collective-permute-start.4) | collective-permute-done | bytes 131104 | tf_op jit(solution)/shard_map/ppermute | solution.py:255
  43.0 1.3 %collective-permute-done.5.corner = f32[256,128]{1,0:T(8,128)S(1)} collective-permute-done((f32[256,128]{1,0:T(8,128)S(1)}, f32[256,128]{1,0:T(8,128)S(1)}, u32[]{:S(2)}, u32[]{:S(2)}) %collective-permute-start.5) | collective-permute-done | bytes 131104 | tf_op jit(solution)/shard_map/ppermute | solution.py:288
  44.3 0.0 copy-start.1
  44.3 2.2 %copy-done.1 = bf16[2,1024,1024]{2,1,0:T(8,128)(2,1)S(1)} copy-done((bf16[2,1024,1024]{2,1,0:T(8,128)(2,1)S(1)}, bf16[2,1024,1024]{2,1,0:T(8,128)(2,1)}, u32[]{:S(2)}) %copy-start.1) | copy-done | bytes 4194328
  46.5 3.3 %pair_fields.1.gradient_ref = f32[256,128]{1,0:T(8,128)S(1)} custom-call(s32[1]{0:T(128)} %bitcast.1.x_ref, f32[256,128]{1,0:T(8,128)S(1)} %bitcast.12, f32[256,128]{1,0:T(8,128)S(1)} %copy-done.4, f32[256,128]{1,0:T(8,128)S(1)} %collective-permute-done.1.below, f32[256,128]{1,0:T(8,128)S(1)} %collective-permute-done.2.above, ...), custom_call_target="tpu_custom_call" | custom-call | flops 1073741824 | bytes 8388608 | tf_op jit(solution)/shard_map/pair_fields/pallas_call | solution.py:227
  49.8 1.1 %overlaps.1 = (f32[32,12,128]{2,1,0:T(8,128)}, f32[8,128]{1,0:T(8,128)S(1)}, bf16[128,1024]{1,0:T(8,128)(2,1)S(1)}, bf16[128,1024]{1,0:T(8,128)(2,1)S(1)}) custom-call(f32[4,264,128]{2,1,0:T(8,128)S(1)} %all-to-all-done.1.gathered_ref, f32[256,128]{1,0:T(8,128)S(1)} %pair_fields.1.gradient_ref), custom_call_target="tpu_custom_call" | custom-call | flops 1073741824 | bytes 8388608 | tf_op jit(solution)/shard_map/overlaps/pallas_call | solution.py:227
  50.9 5.7 %all-to-all-start.2 = ((f32[32,12,128]{2,1,0:T(8,128)}), f32[32,12,128]{2,1,0:T(8,128)S(1)}, u32[]{:S(2)}, u32[]{:S(2)}) async-start(f32[32,12,128]{2,1,0:T(8,128)} %get-tuple-element.26), calls=%async_computation.2 | async-start | bytes 524288 | tf_op jit(solution)/shard_map/all_to_all | solution.py:242
  56.7 0.1 collective-permute-start.6
  56.8 1.1 %collective-permute-done.6.other_ref = f32[8,128]{1,0:T(8,128)S(1)} collective-permute-done((f32[8,128]{1,0:T(8,128)S(1)}, f32[8,128]{1,0:T(8,128)S(1)}, u32[]{:S(2)}, u32[]{:S(2)}) %collective-permute-start.6) | collective-permute-done | bytes 4128 | tf_op jit(solution)/shard_map/ppermute | solution.py:255
  57.9 6.6 %all-to-all-done.2.slabs_ref = f32[32,12,128]{2,1,0:T(8,128)S(1)} async-done(((f32[32,12,128]{2,1,0:T(8,128)}), f32[32,12,128]{2,1,0:T(8,128)S(1)}, u32[]{:S(2)}, u32[]{:S(2)}) %all-to-all-start.2) | async-done | bytes 196640 | tf_op jit(solution)/shard_map/all_to_all | solution.py:242
  64.5 0.3 correlations.1
  64.8 14.4 %all_to_all.26.corr_ref = f32[32,36,128]{2,1,0:T(8,128)S(1)} all-to-all(f32[32,36,128]{2,1,0:T(8,128)S(1)} %get-tuple-element.30), channel_id=1, replica_groups=mesh['spin'=2,'y'=4,'zh'=4,'zl'=2,'x'=4] {'zl','x','y'}, dimensions={0} | all-to-all | bytes 1179648 | tf_op jit(solution)/shard_map/all_to_all | solution.py:242
  79.2 0.4 removal.1
  79.6 12.8 %all_to_all.27 = f32[32,8,128]{2,1,0:T(8,128)S(1)} all-to-all(f32[32,8,128]{2,1,0:T(8,128)S(1)} %removal.1), channel_id=1, replica_groups=mesh['spin'=2,'y'=4,'zh'=4,'zl'=2,'x'=4] {'zl','x','y'}, dimensions={0} | all-to-all | bytes 262144 | tf_op jit(solution)/shard_map/all_to_all | solution.py:242
  92.4 0.7 update.1
  (7 shorter events, 0.0 us)
Async XLA Ops:
  0.6 56.1 %copy-start = (f32[32768]{0:T(1024)S(1)}, f32[32768]{0:T(1024)}, u32[]{:S(2)}) copy-start(f32[32768]{0:T(1024)} %param.5) | copy-start | bytes 393220
  0.6 43.7 %copy-start.2 = (f32[1,1,32768]{2,1,0:T(1,128)S(1)}, f32[1,1,32768]{2,1,0:T(1,128)}, u32[]{:S(2)}) copy-start(f32[1,1,32768]{2,1,0:T(1,128)} %param.4) | copy-start | bytes 393220
  0.7 43.7 %copy-start.3 = (bf16[2,128,128]{2,1,0:T(8,128)(2,1)S(1)}, bf16[2,128,128]{2,1,0:T(8,128)(2,1)}, u32[]{:S(2)}) copy-start(bf16[2,128,128]{2,1,0:T(8,128)(2,1)} %constant.28.clone.lines_ref) | copy-start | bytes 196612
  0.7 16.7 %collective-permute-start = (f32[256,128]{1,0:T(8,128)}, f32[256,128]{1,0:T(8,128)S(1)}, u32[]{:S(2)}, u32[]{:S(2)}) collective-permute-start(f32[256,128]{1,0:T(8,128)} %bitcast.7), channel_id=1, source_target_pairs={{0,124},{1,125},{2,6},{3,7},{4,0},{5,1},{6,10},{7,11},{8,4},{9,5},... | collective-permute-start | bytes 393224 | tf_op jit(solution)/shard_map/ppermute | solution.py:268
  9.1 8.3 %collective-permute-start.1 = (f32[256,128]{1,0:T(8,128)}, f32[256,128]{1,0:T(8,128)S(1)}, u32[]{:S(2)}, u32[]{:S(2)}) collective-permute-start(f32[256,128]{1,0:T(8,128)} %bitcast.8), channel_id=1, source_target_pairs={{0,1},{1,2},{2,3},{3,0},{4,5},{5,6},{6,7},{7,4},{8,9},{9,10},{10,1... | collective-permute-start | bytes 393224 | tf_op jit(solution)/shard_map/ppermute | solution.py:255
  9.1 8.3 %collective-permute-start.2 = (f32[256,128]{1,0:T(8,128)}, f32[256,128]{1,0:T(8,128)S(1)}, u32[]{:S(2)}, u32[]{:S(2)}) collective-permute-start(f32[256,128]{1,0:T(8,128)} %bitcast.9), channel_id=1, source_target_pairs={{0,3},{1,0},{2,1},{3,2},{4,7},{5,4},{6,5},{7,6},{8,11},{9,8},{10,9... | collective-permute-start | bytes 393224 | tf_op jit(solution)/shard_map/ppermute | solution.py:255
  11.1 6.7 %collective-permute-start.3 = (f32[256,128]{1,0:T(8,128)}, f32[256,128]{1,0:T(8,128)S(1)}, u32[]{:S(2)}, u32[]{:S(2)}) collective-permute-start(f32[256,128]{1,0:T(8,128)} %bitcast.10), channel_id=1, source_target_pairs={{0,2},{1,3},{2,0},{3,1},{4,6},{5,7},{6,4},{7,5},{8,10},{9,11},{10,... | collective-permute-start | bytes 393224 | tf_op jit(solution)/shard_map/ppermute | solution.py:255
  17.3 27.0 %copy-start.4 = (f32[256,128]{1,0:T(8,128)S(1)}, f32[256,128]{1,0:T(8,128)}, u32[]{:S(2)}) copy-start(f32[256,128]{1,0:T(8,128)} %get-tuple-element.20.start_ref) | copy-start | bytes 393220
  32.4 17.4 %all-to-all-start.1 = ((f32[4,264,128]{2,1,0:T(8,128)}), f32[4,264,128]{2,1,0:T(8,128)S(1)}, u32[]{:S(2)}, u32[]{:S(2)}) async-start(f32[4,264,128]{2,1,0:T(8,128)} %spread.1), calls=%async_computation.1 | async-start | bytes 1081344 | tf_op jit(solution)/shard_map/all_to_all | solution.py:242
  36.4 6.6 %collective-permute-start.4 = (f32[256,128]{1,0:T(8,128)S(1)}, f32[256,128]{1,0:T(8,128)S(1)}, u32[]{:S(2)}, u32[]{:S(2)}) collective-permute-start(f32[256,128]{1,0:T(8,128)S(1)} %collective-permute-done), channel_id=1, source_target_pairs={{0,2},{1,3},{2,0},{3,1},{4,6},{5,7},{6,4},{7,5},{8,10},{9,11},{10,... | collective-permute-start | bytes 393224 | tf_op jit(solution)/shard_map/ppermute | solution.py:255
  38.1 6.2 %collective-permute-start.5 = (f32[256,128]{1,0:T(8,128)S(1)}, f32[256,128]{1,0:T(8,128)S(1)}, u32[]{:S(2)}, u32[]{:S(2)}) collective-permute-start(f32[256,128]{1,0:T(8,128)S(1)} %collective-permute-done), channel_id=1, source_target_pairs={{0,3},{1,2},{2,1},{3,0},{4,7},{5,6},{6,5},{7,4},{8,11},{9,10},{10,... | collective-permute-start | bytes 393224 | tf_op jit(solution)/shard_map/ppermute | solution.py:288
  44.3 2.2 %copy-start.1 = (bf16[2,1024,1024]{2,1,0:T(8,128)(2,1)S(1)}, bf16[2,1024,1024]{2,1,0:T(8,128)(2,1)}, u32[]{:S(2)}) copy-start(bf16[2,1024,1024]{2,1,0:T(8,128)(2,1)} %constant.27.clone.joined_ref) | copy-start | bytes 12582916
  50.9 13.6 %all-to-all-start.2 = ((f32[32,12,128]{2,1,0:T(8,128)}), f32[32,12,128]{2,1,0:T(8,128)S(1)}, u32[]{:S(2)}, u32[]{:S(2)}) async-start(f32[32,12,128]{2,1,0:T(8,128)} %get-tuple-element.26), calls=%async_computation.2 | async-start | bytes 524288 | tf_op jit(solution)/shard_map/all_to_all | solution.py:242
  56.7 1.3 %collective-permute-start.6 = (f32[8,128]{1,0:T(8,128)S(1)}, f32[8,128]{1,0:T(8,128)S(1)}, u32[]{:S(2)}, u32[]{:S(2)}) collective-permute-start(f32[8,128]{1,0:T(8,128)S(1)} %get-tuple-element.27.square_ref), channel_id=1, source_target_pairs={{0,128},{128,0},{1,129},{129,1},{2,130},{130,2},{3,131},{131,3},{4... | collective-permute-start | bytes 12296 | tf_op jit(solution)/shard_map/ppermute | solution.py:255

commit v4 on v3

--- a/solution.py
+++ b/solution.py
@@ -90,15 +90,18 @@
     return both[:rows] + both[rows:] + mm(line_high, low)
 
 
-def twice_transformed(fields, factors, joined, lines, copies):
-    high, low = split(fields)
+def twice_transformed(fields, factors, joined, lines, copies=()):
+    for copy in copies[:1]:
+        copy.wait()
+    value = along_line(fields, lines)
+    high, low = split(value)
     rows = fields.shape[0]
-    copies[0].wait()
+    for copy in copies[1:2]:
+        copy.wait()
     both = mm(jnp.concatenate([high, low], axis=0), joined[0])
-    copies[1].wait()
-    value = both[:rows] + both[rows:] + mm(high, joined[1])
-    copies[2].wait()
-    value = along_line(value, lines) * factors
+    for copy in copies[2:]:
+        copy.wait()
+    value = (both[:rows] + both[rows:] + mm(high, joined[1])) * factors
     return along_line(product(value, joined[0], joined[1], mm), lines)
 
 
@@ -108,9 +111,9 @@
 
 def table_copies(joined_ref, lines_ref, joined, lines, sems):
     copies = [
-        pltpu.make_async_copy(joined_ref.at[0], joined.at[0], sems.at[0]),
-        pltpu.make_async_copy(joined_ref.at[1], joined.at[1], sems.at[1]),
-        pltpu.make_async_copy(lines_ref, lines, sems.at[2]),
+        pltpu.make_async_copy(lines_ref, lines, sems.at[0]),
+        pltpu.make_async_copy(joined_ref.at[0], joined.at[0], sems.at[1]),
+        pltpu.make_async_copy(joined_ref.at[1], joined.at[1], sems.at[2]),
     ]
     for copy in copies:
         copy.start()
@@ -143,8 +146,7 @@
             packed_ref[k, 1, pl.ds(j, planes, stride=SPLIT), :] = piece[k * planes : (k + 1) * planes]
 
 
-def pair_kernel(x_ref, o_ref, start_ref, below, above, second, across, corner, joined_ref, lines_ref, out_ref, joined, lines, sems):
-    copies = table_copies(joined_ref, lines_ref, joined, lines, sems)
+def pair_kernel(x_ref, o_ref, start_ref, below, above, second, across, corner, joined, lines, out_ref):
     own = to_planes(o_ref)
     below, above, second, across, corner = (to_planes(ref) for ref in (below, above, second, across, corner))
     x = x_ref[0]
@@ -156,7 +158,7 @@
     ]
     fields = jnp.concatenate([own * partner for partner in partners], axis=0)
     factors = jnp.concatenate([screening(wave_square())] * 4, axis=0)
-    fields = twice_transformed(fields, factors, joined, lines, copies)
+    fields = twice_transformed(fields, factors, joined, lines)
     total = sum(fields[k * GRID : (k + 1) * GRID] * partners[k] for k in range(4))
     for j in range(SPLIT):
         rows = pl.ds(j, GRID, stride=SPLIT)
@@ -289,9 +291,8 @@
     gradient = call(
         pair_kernel,
         ((ROWS, LANES), f32),
-        [lax.axis_index("x").reshape(1), own, start, below, above, second, across, corner],
+        [lax.axis_index("x").reshape(1), own, start, below, above, second, across, corner, *tables],
         "pair_fields",
-        tables,
     )
 
     bands = parts * groups

time: 94 us -> 93.1 us (level)
  Pallas kernels: 12.3 us -> 11.2 us
  waiting for transfers between devices: 13 us -> 14.1 us
    pallas_call x7, Pallas kernels: 12.3 us -> 11.2 us  [call(): pl.pallas_call(kernel, out_shape=[jax.ShapeDtypeStruct(s, t) for s, t in...]
  transfers between devices with their start and end apart: 9 -> 9, of which waited for: 5 -> 6; matrix products, arithmetic and copies ran while one was open for 0% -> 0% of each run, Pallas kernels for 10% -> 8%
where the time goes in v4:
time: 93.1 us; the launch traced here: 92.6 us
  blocking collectives  40.6 us (44%)
  starting transfers between devices  23.7 us (25%)
  waiting for transfers between devices  14.1 us (15%)
  Pallas kernels  11.2 us (12%)
  local copies, waits for them, and re-layouts  2.22 us (2%)
    all_to_all x3, blocking collectives, exchange(): return lax.all_to_all(x, axes, 0, 0, tiled=True)  40.6 us
    pallas_call x7, Pallas kernels, call(): pl.pallas_call(kernel, out_shape=[jax.ShapeDtypeStruct(s, t) for s, t in...  11.2 us
    all_to_all x2, starting transfers between devices, exchange(): return lax.all_to_all(x, axes, 0, 0, tiled=True)  9.6 us
    ppermute x1, starting transfers between devices, per_device(): lax.ppermute(own, BANDS, [(g * GRID_X + x, (g + toward[x]) % rings * GRID...  8.38 us
    all_to_all x2, waiting for transfers between devices, exchange(): return lax.all_to_all(x, axes, 0, 0, tiled=True)  7.39 us
    ppermute x5, waiting for transfers between devices, shifted(): return lax.ppermute(x, axes, [(i, (i + by) % peers) for i in range(peers)])  5.4 us
    ppermute x5, starting transfers between devices, shifted(): return lax.ppermute(x, axes, [(i, (i + by) % peers) for i in range(peers)])  4.37 us
    unnamed x10, local copies, waits for them, and re-layouts  2.21 us
  transfers between devices with their start and end apart: 9, of which 6 were waited for; matrix products, arithmetic and copies ran while one was open for 0% of the time, Pallas kernels for 8%

profile of v4, /device:TPU:2, one launch (start us, length us, event | category | flops | bytes accessed | tf_op | source)
XLA Modules:
  0.0 92.6 jit_solution(6229383120645778051)
XLA Ops:
  0.6 0.0 copy-start
  0.7 0.0 copy-start.3
  0.7 8.4 %collective-permute-start = (f32[256,128]{1,0:T(8,128)}, f32[256,128]{1,0:T(8,128)S(1)}, u32[]{:S(2)}, u32[]{:S(2)}) collective-permute-start(f32[256,128]{1,0:T(8,128)} %bitcast.7), channel_id=1, source_target_pairs={{0,124},{1,125},{2,6},{3,7},{4,0},{5,1},{6,10},{7,11},{8,4},{9,5},... | collective-permute-start | bytes 393224 | tf_op jit(solution)/shard_map/ppermute | solution.py:270
  9.1 0.0 collective-permute-start.1
  9.1 2.0 %collective-permute-start.2 = (f32[256,128]{1,0:T(8,128)}, f32[256,128]{1,0:T(8,128)S(1)}, u32[]{:S(2)}, u32[]{:S(2)}) collective-permute-start(f32[256,128]{1,0:T(8,128)} %bitcast.9), channel_id=1, source_target_pairs={{0,3},{1,0},{2,1},{3,2},{4,7},{5,4},{6,5},{7,6},{8,11},{9,8},{10,9... | collective-permute-start | bytes 393224 | tf_op jit(solution)/shard_map/ppermute | solution.py:257
  11.1 0.6 collective-permute-start.3
  11.7 5.4 %own_fields.1 = (f32[32,2,8,128]{3,2,1,0:T(8,128)}, f32[256,128]{1,0:T(8,128)}) custom-call(f32[256,128]{1,0:T(8,128)} %bitcast.11, bf16[2,1024,1024]{2,1,0:T(8,128)(2,1)} %constant.27.clone.joined_ref.joined, bf16[2,128,128]{2,1,0:T(8,128)(2,1)} %constant.28.clone.lines_ref.lines), custom_call_target="tpu_custom_call" | custom-call | flops 1073741824 | bytes 8388608 | tf_op jit(solution)/shard_map/own_fields/pallas_call | solution.py:229
  17.0 0.0 copy-start.4
  17.1 0.0 collective-permute-done
  17.1 0.0 collective-permute-done.1.below
  17.1 0.7 collective-permute-done.3.second
  17.8 13.5 %all_to_all.25.slabs_ref.own_ref = f32[32,2,8,128]{3,2,1,0:T(8,128)S(1)} all-to-all(f32[32,2,8,128]{3,2,1,0:T(8,128)} %get-tuple-element.19), channel_id=1, replica_groups=mesh['spin'=2,'y'=4,'zh'=4,'zl'=2,'x'=4] {'zl','x','y'}, dimensions={0} | all-to-all | bytes 524288 | tf_op jit(solution)/shard_map/all_to_all | solution.py:244
  31.3 0.9 spread.1
  32.1 4.2 %all-to-all-start.1 = ((f32[4,264,128]{2,1,0:T(8,128)}), f32[4,264,128]{2,1,0:T(8,128)S(1)}, u32[]{:S(2)}, u32[]{:S(2)}) async-start(f32[4,264,128]{2,1,0:T(8,128)} %spread.1), calls=%async_computation.1 | async-start | bytes 1081344 | tf_op jit(solution)/shard_map/all_to_all | solution.py:244
  36.4 1.7 %collective-permute-start.4 = (f32[256,128]{1,0:T(8,128)S(1)}, f32[256,128]{1,0:T(8,128)S(1)}, u32[]{:S(2)}, u32[]{:S(2)}) collective-permute-start(f32[256,128]{1,0:T(8,128)S(1)} %collective-permute-done), channel_id=1, source_target_pairs={{0,2},{1,3},{2,0},{3,1},{4,6},{5,7},{6,4},{7,5},{8,10},{9,11},{10,... | collective-permute-start | bytes 393224 | tf_op jit(solution)/shard_map/ppermute | solution.py:257
  38.0 1.3 %collective-permute-start.5 = (f32[256,128]{1,0:T(8,128)S(1)}, f32[256,128]{1,0:T(8,128)S(1)}, u32[]{:S(2)}, u32[]{:S(2)}) collective-permute-start(f32[256,128]{1,0:T(8,128)S(1)} %collective-permute-done), channel_id=1, source_target_pairs={{0,3},{1,2},{2,1},{3,0},{4,7},{5,6},{6,5},{7,4},{8,11},{9,10},{10,... | collective-permute-start | bytes 393224 | tf_op jit(solution)/shard_map/ppermute | solution.py:290
  39.3 3.6 %collective-permute-done.4.across = f32[256,128]{1,0:T(8,128)S(1)} collective-permute-done((f32[256,128]{1,0:T(8,128)S(1)}, f32[256,128]{1,0:T(8,128)S(1)}, u32[]{:S(2)}, u32[]{:S(2)}) %collective-permute-start.4) | collective-permute-done | bytes 131104 | tf_op jit(solution)/shard_map/ppermute | solution.py:257
  42.9 1.3 %collective-permute-done.5.corner = f32[256,128]{1,0:T(8,128)S(1)} collective-permute-done((f32[256,128]{1,0:T(8,128)S(1)}, f32[256,128]{1,0:T(8,128)S(1)}, u32[]{:S(2)}, u32[]{:S(2)}) %collective-permute-start.5) | collective-permute-done | bytes 131104 | tf_op jit(solution)/shard_map/ppermute | solution.py:290
  44.2 0.0 copy-start.1
  44.3 2.2 %copy-done.1 = bf16[2,1024,1024]{2,1,0:T(8,128)(2,1)S(1)} copy-done((bf16[2,1024,1024]{2,1,0:T(8,128)(2,1)S(1)}, bf16[2,1024,1024]{2,1,0:T(8,128)(2,1)}, u32[]{:S(2)}) %copy-start.1) | copy-done | bytes 4194328
  46.4 2.4 %pair_fields.1.gradient_ref = f32[256,128]{1,0:T(8,128)S(1)} custom-call(s32[1]{0:T(128)} %bitcast.1.x_ref, f32[256,128]{1,0:T(8,128)S(1)} %bitcast.12, f32[256,128]{1,0:T(8,128)S(1)} %copy-done.4, f32[256,128]{1,0:T(8,128)S(1)} %collective-permute-done.1.below, f32[256,128]{1,0:T(8,128)S(1)} %collective-permute-done.2.above, ...), custom_call_target="tpu_custom_call" | custom-call | flops 1073741824 | bytes 8388608 | tf_op jit(solution)/shard_map/pair_fields/pallas_call | solution.py:229
  48.9 0.8 all-to-all-done.1.gathered_ref
  49.7 1.1 %overlaps.1 = (f32[32,12,128]{2,1,0:T(8,128)}, f32[8,128]{1,0:T(8,128)S(1)}, bf16[128,1024]{1,0:T(8,128)(2,1)S(1)}, bf16[128,1024]{1,0:T(8,128)(2,1)S(1)}) custom-call(f32[4,264,128]{2,1,0:T(8,128)S(1)} %all-to-all-done.1.gathered_ref, f32[256,128]{1,0:T(8,128)S(1)} %pair_fields.1.gradient_ref), custom_call_target="tpu_custom_call" | custom-call | flops 1073741824 | bytes 8388608 | tf_op jit(solution)/shard_map/overlaps/pallas_call | solution.py:229
  50.8 5.4 %all-to-all-start.2 = ((f32[32,12,128]{2,1,0:T(8,128)}), f32[32,12,128]{2,1,0:T(8,128)S(1)}, u32[]{:S(2)}, u32[]{:S(2)}) async-start(f32[32,12,128]{2,1,0:T(8,128)} %get-tuple-element.26), calls=%async_computation.2 | async-start | bytes 524288 | tf_op jit(solution)/shard_map/all_to_all | solution.py:244
  56.2 0.1 collective-permute-start.6
  56.3 1.1 %collective-permute-done.6.other_ref = f32[8,128]{1,0:T(8,128)S(1)} collective-permute-done((f32[8,128]{1,0:T(8,128)S(1)}, f32[8,128]{1,0:T(8,128)S(1)}, u32[]{:S(2)}, u32[]{:S(2)}) %collective-permute-start.6) | collective-permute-done | bytes 4128 | tf_op jit(solution)/shard_map/ppermute | solution.py:257
  57.5 6.6 %all-to-all-done.2.slabs_ref = f32[32,12,128]{2,1,0:T(8,128)S(1)} async-done(((f32[32,12,128]{2,1,0:T(8,128)}), f32[32,12,128]{2,1,0:T(8,128)S(1)}, u32[]{:S(2)}, u32[]{:S(2)}) %all-to-all-start.2) | async-done | bytes 196640 | tf_op jit(solution)/shard_map/all_to_all | solution.py:244
  64.0 0.3 correlations.1
  64.3 14.4 %all_to_all.26.corr_ref = f32[32,36,128]{2,1,0:T(8,128)S(1)} all-to-all(f32[32,36,128]{2,1,0:T(8,128)S(1)} %get-tuple-element.30), channel_id=1, replica_groups=mesh['spin'=2,'y'=4,'zh'=4,'zl'=2,'x'=4] {'zl','x','y'}, dimensions={0} | all-to-all | bytes 1179648 | tf_op jit(solution)/shard_map/all_to_all | solution.py:244
  78.7 0.4 removal.1
  79.2 12.8 %all_to_all.27 = f32[32,8,128]{2,1,0:T(8,128)S(1)} all-to-all(f32[32,8,128]{2,1,0:T(8,128)S(1)} %removal.1), channel_id=1, replica_groups=mesh['spin'=2,'y'=4,'zh'=4,'zl'=2,'x'=4] {'zl','x','y'}, dimensions={0} | all-to-all | bytes 262144 | tf_op jit(solution)/shard_map/all_to_all | solution.py:244
  91.9 0.7 update.1
  (7 shorter events, 0.0 us)
Async XLA Ops:
  0.6 55.7 %copy-start = (f32[32768]{0:T(1024)S(1)}, f32[32768]{0:T(1024)}, u32[]{:S(2)}) copy-start(f32[32768]{0:T(1024)} %param.5) | copy-start | bytes 393220
  0.6 43.6 %copy-start.2 = (f32[1,1,32768]{2,1,0:T(1,128)S(1)}, f32[1,1,32768]{2,1,0:T(1,128)}, u32[]{:S(2)}) copy-start(f32[1,1,32768]{2,1,0:T(1,128)} %param.4) | copy-start | bytes 393220
  0.7 43.6 %copy-start.3 = (bf16[2,128,128]{2,1,0:T(8,128)(2,1)S(1)}, bf16[2,128,128]{2,1,0:T(8,128)(2,1)}, u32[]{:S(2)}) copy-start(bf16[2,128,128]{2,1,0:T(8,128)(2,1)} %constant.28.clone.lines_ref.lines) | copy-start | bytes 196612
  0.7 16.4 %collective-permute-start = (f32[256,128]{1,0:T(8,128)}, f32[256,128]{1,0:T(8,128)S(1)}, u32[]{:S(2)}, u32[]{:S(2)}) collective-permute-start(f32[256,128]{1,0:T(8,128)} %bitcast.7), channel_id=1, source_target_pairs={{0,124},{1,125},{2,6},{3,7},{4,0},{5,1},{6,10},{7,11},{8,4},{9,5},... | collective-permute-start | bytes 393224 | tf_op jit(solution)/shard_map/ppermute | solution.py:270
  9.1 8.0 %collective-permute-start.1 = (f32[256,128]{1,0:T(8,128)}, f32[256,128]{1,0:T(8,128)S(1)}, u32[]{:S(2)}, u32[]{:S(2)}) collective-permute-start(f32[256,128]{1,0:T(8,128)} %bitcast.8), channel_id=1, source_target_pairs={{0,1},{1,2},{2,3},{3,0},{4,5},{5,6},{6,7},{7,4},{8,9},{9,10},{10,1... | collective-permute-start | bytes 393224 | tf_op jit(solution)/shard_map/ppermute | solution.py:257
  9.1 8.0 %collective-permute-start.2 = (f32[256,128]{1,0:T(8,128)}, f32[256,128]{1,0:T(8,128)S(1)}, u32[]{:S(2)}, u32[]{:S(2)}) collective-permute-start(f32[256,128]{1,0:T(8,128)} %bitcast.9), channel_id=1, source_target_pairs={{0,3},{1,0},{2,1},{3,2},{4,7},{5,4},{6,5},{7,6},{8,11},{9,8},{10,9... | collective-permute-start | bytes 393224 | tf_op jit(solution)/shard_map/ppermute | solution.py:257
  11.1 6.7 %collective-permute-start.3 = (f32[256,128]{1,0:T(8,128)}, f32[256,128]{1,0:T(8,128)S(1)}, u32[]{:S(2)}, u32[]{:S(2)}) collective-permute-start(f32[256,128]{1,0:T(8,128)} %bitcast.10), channel_id=1, source_target_pairs={{0,2},{1,3},{2,0},{3,1},{4,6},{5,7},{6,4},{7,5},{8,10},{9,11},{10,... | collective-permute-start | bytes 393224 | tf_op jit(solution)/shard_map/ppermute | solution.py:257
  17.0 27.2 %copy-start.4 = (f32[256,128]{1,0:T(8,128)S(1)}, f32[256,128]{1,0:T(8,128)}, u32[]{:S(2)}) copy-start(f32[256,128]{1,0:T(8,128)} %get-tuple-element.20.start_ref) | copy-start | bytes 393220
  32.1 17.6 %all-to-all-start.1 = ((f32[4,264,128]{2,1,0:T(8,128)}), f32[4,264,128]{2,1,0:T(8,128)S(1)}, u32[]{:S(2)}, u32[]{:S(2)}) async-start(f32[4,264,128]{2,1,0:T(8,128)} %spread.1), calls=%async_computation.1 | async-start | bytes 1081344 | tf_op jit(solution)/shard_map/all_to_all | solution.py:244
  36.4 6.6 %collective-permute-start.4 = (f32[256,128]{1,0:T(8,128)S(1)}, f32[256,128]{1,0:T(8,128)S(1)}, u32[]{:S(2)}, u32[]{:S(2)}) collective-permute-start(f32[256,128]{1,0:T(8,128)S(1)} %collective-permute-done), channel_id=1, source_target_pairs={{0,2},{1,3},{2,0},{3,1},{4,6},{5,7},{6,4},{7,5},{8,10},{9,11},{10,... | collective-permute-start | bytes 393224 | tf_op jit(solution)/shard_map/ppermute | solution.py:257
  38.0 6.2 %collective-permute-start.5 = (f32[256,128]{1,0:T(8,128)S(1)}, f32[256,128]{1,0:T(8,128)S(1)}, u32[]{:S(2)}, u32[]{:S(2)}) collective-permute-start(f32[256,128]{1,0:T(8,128)S(1)} %collective-permute-done), channel_id=1, source_target_pairs={{0,3},{1,2},{2,1},{3,0},{4,7},{5,6},{6,5},{7,4},{8,11},{9,10},{10,... | collective-permute-start | bytes 393224 | tf_op jit(solution)/shard_map/ppermute | solution.py:290
  44.2 2.2 %copy-start.1 = (bf16[2,1024,1024]{2,1,0:T(8,128)(2,1)S(1)}, bf16[2,1024,1024]{2,1,0:T(8,128)(2,1)}, u32[]{:S(2)}) copy-start(bf16[2,1024,1024]{2,1,0:T(8,128)(2,1)} %constant.27.clone.joined_ref.joined) | copy-start | bytes 12582916
  50.8 13.2 %all-to-all-start.2 = ((f32[32,12,128]{2,1,0:T(8,128)}), f32[32,12,128]{2,1,0:T(8,128)S(1)}, u32[]{:S(2)}, u32[]{:S(2)}) async-start(f32[32,12,128]{2,1,0:T(8,128)} %get-tuple-element.26), calls=%async_computation.2 | async-start | bytes 524288 | tf_op jit(solution)/shard_map/all_to_all | solution.py:244
  56.2 1.3 %collective-permute-start.6 = (f32[8,128]{1,0:T(8,128)S(1)}, f32[8,128]{1,0:T(8,128)S(1)}, u32[]{:S(2)}, u32[]{:S(2)}) collective-permute-start(f32[8,128]{1,0:T(8,128)S(1)} %get-tuple-element.27.square_ref), channel_id=1, source_target_pairs={{0,128},{128,0},{1,129},{129,1},{2,130},{130,2},{3,131},{131,3},{4... | collective-permute-start | bytes 12296 | tf_op jit(solution)/shard_map/ppermute | solution.py:257
